TPU v7x, 32 devices: a whole 2x2x4 slice. The times are simulated.
32 devices in a mesh: dp: 16 (over z, x, core), lon: 2 (over y).
Axes of the slice: x: 2, y: 2, z: 4, core: 2. Of those that a mesh axis runs over, the one named last changes fastest.
Arguments:
- features: bfloat16 [16, 18, 48, 1152], P('dp', 'lon'), may hold values from -6 to 6
- depth_w: bfloat16 [2, 3, 3, 1152], replicated, may hold values from -2 to 2
- point_w: bfloat16 [2, 1152, 256], replicated, may hold values from -0.1875 to 0.1875
- point_bias: float32 [2, 256], replicated, may hold values from -3 to 3
- cotangent: bfloat16 [16, 18, 48, 512], P('dp', 'lon'), may hold values from -6 to 6
Outputs:
- feature_grad: bfloat16 [16, 18, 48, 1152], P('dp', 'lon')
- depth_grad: bfloat16 [2, 3, 3, 1152], replicated
- point_grad: bfloat16 [2, 1152, 256], replicated
- bias_grad: float32 [2, 256], replicated
All inputs are finite; a program needn't handle non-finite values.
Results may differ from a plain program's by a relative error of at most 0.0075.
Values may be sent and summed in bfloat16 or wider, within the bound.
A program may use at most 128 MiB of HBM per device.

v0:
```python
import jax
import jax.numpy as jnp
from jax import lax
from jax.sharding import PartitionSpec as P

RATE_A = 24
RATE_B = 36


def from_behind(block, axis, distance):
    devices = range(lax.axis_size(axis))
    route = [((i - distance) % len(devices), i) for i in devices]
    return lax.ppermute(block, axis, route)


def lat_shift(grid_field, offset, axis_pos):
    height = grid_field.shape[axis_pos]
    if offset == 0:
        return grid_field
    widths = [(0, 0)] * grid_field.ndim
    if offset > 0:
        kept_rows = lax.slice_in_dim(grid_field, offset, height, axis=axis_pos)
        widths[axis_pos] = (0, offset)
    else:
        kept_rows = lax.slice_in_dim(grid_field, 0, height + offset, axis=axis_pos)
        widths[axis_pos] = (-offset, 0)
    return jnp.pad(kept_rows, widths)


def gate_slope(pre_act):
    sigmoid_val = jax.nn.sigmoid(pre_act)
    return sigmoid_val * (1.0 + pre_act * (1.0 - sigmoid_val))


def column_plan(dilation, direction, columns, group_size):
    run_list = []
    for column in range(columns):
        target = column + direction * dilation
        offset = target // columns
        local_col = target % columns
        if run_list and run_list[-1][0] == offset:
            run_list[-1][2] = local_col + 1
        else:
            run_list.append([offset, local_col, local_col + 1])
    return [(-entry[0] % group_size, entry[1], entry[2]) for entry in run_list]


def join_pieces(piece_list):
    if len(piece_list) == 1:
        return piece_list[0]
    return jnp.concatenate(piece_list, axis=1)


def fetch_each(grid_field, offset_pairs, group_size, send_fn):
    result = {}
    for offset_pair in offset_pairs:
        piece_list = []
        for shift_by, first_col, finish in column_plan(
            offset_pair[0], offset_pair[1], grid_field.shape[1], group_size
        ):
            column_piece = grid_field[:, first_col:finish]
            if shift_by != 0:
                column_piece = send_fn(column_piece, shift_by)
            piece_list.append(column_piece)
        result[offset_pair] = join_pieces(piece_list)
    return result


def send_features(column_piece, shift_by):
    return from_behind(column_piece, "lon", shift_by)


def send_grads(column_piece, shift_by):
    return from_behind(column_piece, "lon", shift_by)


def per_device(features, depth_w, point_w, point_bias, cotangent):
    group_size = lax.axis_size("lon")
    channels = features.shape[3]
    outputs = point_w.shape[2]
    dilations = (RATE_A, RATE_B)
    offset_pairs = [(dilation, direction) for dilation in dilations for direction in (-1, 1)]
    moved_in = fetch_each(features, offset_pairs, group_size, send_features)
    depth_outs = []
    for branch, dilation in enumerate(dilations):
        depth_acc = jnp.zeros(features.shape, jnp.float32)
        for lon_step in (-1, 0, 1):
            source = features if lon_step == 0 else moved_in[dilation, lon_step]
            for lat_step in (-1, 0, 1):
                tapped = lat_shift(source, lat_step * dilation, 2).astype(jnp.float32)
                depth_acc = (
                    depth_acc
                    + depth_w[branch, lat_step + 1, lon_step + 1].astype(jnp.float32) * tapped
                )
        depth_outs.append(depth_acc.astype(jnp.bfloat16))
    point_terms = []
    bias_terms = []
    dgrad_list = []
    for branch, dilation in enumerate(dilations):
        flat_depth = depth_outs[branch].reshape(-1, channels)
        point_act = (
            jnp.dot(flat_depth, point_w[branch], preferred_element_type=jnp.float32)
            + point_bias[branch]
        )
        upstream_part = (
            cotangent[..., branch * outputs : (branch + 1) * outputs]
            .reshape(-1, outputs)
            .astype(jnp.float32)
        )
        pgrad = (upstream_part * gate_slope(point_act)).astype(jnp.bfloat16)
        bias_terms.append(jnp.sum(pgrad.astype(jnp.float32), axis=0))
        point_terms.append(
            lax.dot_general(
                flat_depth, pgrad, (((0,), (0,)), ((), ())), preferred_element_type=jnp.float32
            )
        )
        dgrad = lax.dot_general(
            pgrad, point_w[branch], (((1,), (1,)), ((), ())), preferred_element_type=jnp.float32
        )
        dgrad_list.append(dgrad.astype(jnp.bfloat16).reshape(features.shape))
    point_local = jnp.stack(point_terms)
    bias_local = jnp.stack(bias_terms)
    grad_field = jnp.zeros(features.shape, jnp.float32)
    depth_terms = []
    for branch, dilation in enumerate(dilations):
        branch_pairs = [(dilation, -1), (dilation, 1)]
        moved_back = fetch_each(dgrad_list[branch], branch_pairs, group_size, send_grads)
        dgrad_wide = dgrad_list[branch].astype(jnp.float32)
        tap_rows = []
        for lat_step in (-1, 0, 1):
            tap_cols = []
            for lon_step in (-1, 0, 1):
                source = features if lon_step == 0 else moved_in[dilation, lon_step]
                tapped = lat_shift(source, lat_step * dilation, 2).astype(jnp.float32)
                tap_cols.append(jnp.sum(tapped * dgrad_wide, axis=(0, 1, 2)))
                behind = dgrad_list[branch] if lon_step == 0 else moved_back[dilation, -lon_step]
                behind = lat_shift(behind, -lat_step * dilation, 2).astype(jnp.float32)
                grad_field = (
                    grad_field
                    + depth_w[branch, lat_step + 1, lon_step + 1].astype(jnp.float32) * behind
                )
            tap_rows.append(jnp.stack(tap_cols))
        depth_terms.append(jnp.stack(tap_rows))
    depth_local = jnp.stack(depth_terms)
    feature_grad = grad_field.astype(jnp.bfloat16)
    point_sum, depth_sum, bias_sum = lax.psum((point_local, depth_local, bias_local), ("dp", "lon"))
    images = lax.axis_size("dp") * features.shape[0]
    depth_grad = (depth_sum / images).astype(jnp.bfloat16)
    point_grad = (point_sum / images).astype(jnp.bfloat16)
    bias_grad = bias_sum / images
    return (feature_grad, depth_grad, point_grad, bias_grad)


def solution(mesh):
    placed = (P("dp", "lon", None, None), P(), P(), P(), P("dp", "lon", None, None))
    return jax.shard_map(
        per_device,
        mesh=mesh,
        in_specs=placed,
        out_specs=(P("dp", "lon", None, None), P(), P(), P()),
        check_vma=False,
    )
```

profile of v0, /device:TPU:0, one launch (start us, length us, event | category | flops | bytes accessed | tf_op | source)
XLA Modules:
  0.0 272.1 jit_solution(13312511599037007877)
XLA Ops:
  7.2 1.5 fusion.74
  8.7 3.0 %collective-permute-start = (bf16[1,6,48,1152]{3,2,1,0:T(8,128)(2,1)S(1)}, bf16[1,6,48,1152]{3,2,1,0:T(8,128)(2,1)S(1)}, u32[]{:S(2)}, u32[]{:S(2)}) collective-permute-start(bf16[1,6,48,1152]{3,2,1,0:T(8,128)(2,1)S(1)} %get-tuple-element.56), channel_id=1, source_target_pairs={{1,0},{0,1},{3,2},{2,3},{5,4},{4,5},{7,6},{6,7},{9,8},{8,9},{11,10... | collective-permute-start | bytes 1990664 | tf_op jit(solution)/shard_map/ppermute | solution.py:13
  13.0 1.2 fusion.29
  15.4 1.5 convolution_bitcast_fusion
  16.9 0.8 fusion.70
  17.7 9.7 %collective-permute-done = bf16[1,6,48,1152]{3,2,1,0:T(8,128)(2,1)S(1)} collective-permute-done((bf16[1,6,48,1152]{3,2,1,0:T(8,128)(2,1)S(1)}, bf16[1,6,48,1152]{3,2,1,0:T(8,128)(2,1)S(1)}, u32[]{:S(2)}, u32[]{:S(2)}) %collective-permute-start) | collective-permute-done | bytes 663584 | tf_op jit(solution)/shard_map/ppermute | solution.py:13
  27.6 13.3 %collective-permute-done.1 = bf16[1,6,48,1152]{3,2,1,0:T(8,128)(2,1)S(1)} collective-permute-done((bf16[1,6,48,1152]{3,2,1,0:T(8,128)(2,1)S(1)}, bf16[1,6,48,1152]{3,2,1,0:T(8,128)(2,1)S(1)}, u32[]{:S(2)}, u32[]{:S(2)}) %collective-permute-start.1) | collective-permute-done | bytes 663584 | tf_op jit(solution)/shard_map/ppermute | solution.py:13
  41.1 2.2 fusion.8
  43.8 1.6 convolution_bitcast_fusion.1
  45.7 0.6 fusion.9
  46.3 3.7 %fusion.38 = (f32[1152]{0:T(1024)S(1)}, f32[1152]{0:T(1024)S(1)}, f32[1152]{0:T(1024)S(1)}, f32[1152]{0:T(1024)S(1)}, f32[1152]{0:T(1024)}, /*index=5*/f32[1152]...) fusion(bf16[1,9,48,1152]{3,2,1,0:T(8,128)(2,1)S(1)} %bitcast.58, ...), kind=kLoop, calls=%fused_computation.82 | loop fusion | flops 15416064 | bytes 6515712 | tf_op jit(solution)/shard_map/reduce_sum | solution.py:135
  50.0 1.2 fusion.72
  51.1 1.0 fusion.69
  52.2 0.6 stack.100
  57.5 1.7 collective-permute-start.2
  60.2 62.4 %psum.23 = f32[2,256]{1,0:T(2,128)S(1)} all-reduce(f32[2,256]{1,0:T(2,128)} %pad_maximum_fusion.6), channel_id=1, replica_groups=mesh['dp'=16,'lon'=2] {'dp','lon'}, use_global_device_ids=true, to_apply=%region_16.17 | all-reduce | flops 512 | bytes 4096 | tf_op jit(solution)/shard_map/psum | solution.py:146
  122.7 2.9 %pad_maximum_fusion = f32[2,1152,256]{2,1,0:T(8,128)} fusion(f32[1,1152,256]{2,1,0:T(8,128)S(1)} %copy-done.1, f32[1,1152,256]{2,1,0:T(8,128)} %convolution_bitcast_fusion.1), kind=kLoop, calls=%fused_computation.42 | loop fusion | flops 589824 | bytes 4718592 | tf_op jit(solution)/shard_map/stack | solution.py:121
  125.8 0.7 pad_maximum_fusion.5
  127.3 1.3 fusion.57
  128.6 1.2 fusion.55
  130.0 4.9 %fusion.20 = bf16[1,9,48,1152]{3,2,1,0:T(8,128)(2,1)} fusion(bf16[1,9,48,1152]{3,2,1,0:T(8,128)(2,1)S(1)} %bitcast.65, bf16[1,9,48,1152]{3,2,1,0:T(8,128)(2,1)S(1)} %bitcast.62, bf16[1,3,48,1152]{3,2,1,0:T(8,128)(2,1)S(1)} %get-tuple-element.49, bf16[1,6,48,1152]{3,2,1,0:T(8,128)(2,1)} %collective-permute-done.3, ...), kind=kLoop, calls=%fused_computation.64 | loop fusion | flops 26873856 | bytes 8543232 | tf_op jit(solution)/shard_map/convert_element_type | solution.py:145
  134.9 126.7 %all-reduce.19.cloned.1.call-done = (f32[2,3,3,1152]{3,2,1,0:T(4,128)}, f32[2,1152,256]{2,1,0:T(8,128)}) async-done(((f32[2,3,3,1152]{3,2,1,0:T(4,128)}, f32[2,1152,256]{2,1,0:T(8,128)}), (f32[2,3,3,1152]{3,2,1,0:T(4,128)}, f32[2,1152,256]{2,1,0:T(8,128)})) %all-reduce.19.cloned.1.call-update) | async-done | bytes 2442256 | tf_op jit(solution)/shard_map/psum | solution.py:146
  261.6 2.9 %multiply_convert_fusion = bf16[2,1152,256]{2,1,0:T(8,128)(2,1)} fusion(f32[2,1152,256]{2,1,0:T(8,128)} %get-tuple-element.39), kind=kLoop, calls=%fused_computation.43 | loop fusion | flops 1179648 | bytes 3538944 | tf_op jit(solution)/shard_map/convert_element_type | solution.py:149
  264.6 0.7 copy.9
  (130 shorter events, 9.9 us)
Async XLA Ops:
  7.2 4.7 %copy-start = (bf16[1,9,48,1152]{3,2,1,0:T(8,128)(2,1)S(1)}, bf16[1,9,48,1152]{3,2,1,0:T(8,128)(2,1)}, u32[]{:S(2)}) copy-start(bf16[1,9,48,1152]{3,2,1,0:T(8,128)(2,1)} %param.5) | copy-start | bytes 2985988
  7.2 254.4 %all-reduce.19.cloned.1.call-start = ((), (), s32[]{:S(2)}) async-start(), calls=%async_computation | async-start | bytes 4939776 | tf_op jit(solution)/shard_map/psum | solution.py:146
  8.7 18.8 %collective-permute-start = (bf16[1,6,48,1152]{3,2,1,0:T(8,128)(2,1)S(1)}, bf16[1,6,48,1152]{3,2,1,0:T(8,128)(2,1)S(1)}, u32[]{:S(2)}, u32[]{:S(2)}) collective-permute-start(bf16[1,6,48,1152]{3,2,1,0:T(8,128)(2,1)S(1)} %get-tuple-element.56), channel_id=1, source_target_pairs={{1,0},{0,1},{3,2},{2,3},{5,4},{4,5},{7,6},{6,7},{9,8},{8,9},{11,10... | collective-permute-start | bytes 1990664 | tf_op jit(solution)/shard_map/ppermute | solution.py:13
  11.7 29.1 %collective-permute-start.1 = (bf16[1,6,48,1152]{3,2,1,0:T(8,128)(2,1)S(1)}, bf16[1,6,48,1152]{3,2,1,0:T(8,128)(2,1)S(1)}, u32[]{:S(2)}, u32[]{:S(2)}) collective-permute-start(bf16[1,6,48,1152]{3,2,1,0:T(8,128)(2,1)S(1)} %get-tuple-element.57), channel_id=1, source_target_pairs={{1,0},{0,1},{3,2},{2,3},{5,4},{4,5},{7,6},{6,7},{9,8},{8,9},{11,10... | collective-permute-start | bytes 1990664 | tf_op jit(solution)/shard_map/ppermute | solution.py:13
  12.9 28.1 %copy-start.15 = (f32[1152]{0:T(1024)}, f32[1152]{0:T(1024)S(1)}, u32[]{:S(2)}) copy-start(f32[1152]{0:T(1024)S(1)} %get-tuple-element.20) | copy-start | bytes 13828
  12.9 28.1 %copy-start.17 = (f32[1152]{0:T(1024)}, f32[1152]{0:T(1024)S(1)}, u32[]{:S(2)}) copy-start(f32[1152]{0:T(1024)S(1)} %get-tuple-element.28) | copy-start | bytes 13828
  12.9 28.1 %copy-start.19 = (f32[1152]{0:T(1024)}, f32[1152]{0:T(1024)S(1)}, u32[]{:S(2)}) copy-start(f32[1152]{0:T(1024)S(1)} %get-tuple-element.29) | copy-start | bytes 13828
  12.9 28.1 %copy-start.21 = (f32[1152]{0:T(1024)}, f32[1152]{0:T(1024)S(1)}, u32[]{:S(2)}) copy-start(f32[1152]{0:T(1024)S(1)} %get-tuple-element.30) | copy-start | bytes 13828
  12.9 28.1 %copy-start.23 = (f32[1152]{0:T(1024)}, f32[1152]{0:T(1024)S(1)}, u32[]{:S(2)}) copy-start(f32[1152]{0:T(1024)S(1)} %get-tuple-element.31) | copy-start | bytes 13828
  12.9 28.1 %copy-start.25 = (f32[1152]{0:T(1024)}, f32[1152]{0:T(1024)S(1)}, u32[]{:S(2)}) copy-start(f32[1152]{0:T(1024)S(1)} %get-tuple-element.32) | copy-start | bytes 13828
  13.0 28.1 %copy-start.27 = (f32[1152]{0:T(1024)}, f32[1152]{0:T(1024)S(1)}, u32[]{:S(2)}) copy-start(f32[1152]{0:T(1024)S(1)} %get-tuple-element.33) | copy-start | bytes 13828
  13.0 28.1 %copy-start.29 = (f32[1152]{0:T(1024)}, f32[1152]{0:T(1024)S(1)}, u32[]{:S(2)}) copy-start(f32[1152]{0:T(1024)S(1)} %get-tuple-element.34) | copy-start | bytes 13828
  13.0 28.1 %copy-start.31 = (f32[1152]{0:T(1024)}, f32[1152]{0:T(1024)S(1)}, u32[]{:S(2)}) copy-start(f32[1152]{0:T(1024)S(1)} %get-tuple-element.35) | copy-start | bytes 13828
  50.0 72.6 %copy-start.1 = (f32[1,1152,256]{2,1,0:T(8,128)S(1)}, f32[1,1152,256]{2,1,0:T(8,128)}, u32[]{:S(2)}) copy-start(f32[1,1152,256]{2,1,0:T(8,128)} %convolution_bitcast_fusion) | copy-start | bytes 3538948
  57.5 69.6 %collective-permute-start.2 = (bf16[1,6,48,1152]{3,2,1,0:T(8,128)(2,1)}, bf16[1,6,48,1152]{3,2,1,0:T(8,128)(2,1)}, u32[]{:S(2)}, u32[]{:S(2)}) collective-permute-start(bf16[1,6,48,1152]{3,2,1,0:T(8,128)(2,1)} %get-tuple-element.50), channel_id=1, source_target_pairs={{1,0},{0,1},{3,2},{2,3},{5,4},{4,5},{7,6},{6,7},{9,8},{8,9},{11,10... | collective-permute-start | bytes 1990664 | tf_op jit(solution)/shard_map/ppermute | solution.py:13
  59.3 69.3 %collective-permute-start.3 = (bf16[1,6,48,1152]{3,2,1,0:T(8,128)(2,1)}, bf16[1,6,48,1152]{3,2,1,0:T(8,128)(2,1)}, u32[]{:S(2)}, u32[]{:S(2)}) collective-permute-start(bf16[1,6,48,1152]{3,2,1,0:T(8,128)(2,1)} %get-tuple-element.51), channel_id=1, source_target_pairs={{1,0},{0,1},{3,2},{2,3},{5,4},{4,5},{7,6},{6,7},{9,8},{8,9},{11,10... | collective-permute-start | bytes 1990664 | tf_op jit(solution)/shard_map/ppermute | solution.py:13
  122.6 3.1 %copy-start.36 = (f32[1,1152]{1,0:T(1,128)S(1)}, f32[1,1152]{1,0:T(1,128)}, u32[]{:S(2)}) copy-start(f32[1,1152]{1,0:T(1,128)} %stack.100) | copy-start | bytes 13828
  122.6 3.1 %copy-start.37 = (f32[1,1152]{1,0:T(1,128)S(1)}, f32[1,1152]{1,0:T(1,128)}, u32[]{:S(2)}) copy-start(f32[1,1152]{1,0:T(1,128)} %stack.101) | copy-start | bytes 13828
  122.6 3.1 %copy-start.38 = (f32[1,1152]{1,0:T(1,128)S(1)}, f32[1,1152]{1,0:T(1,128)}, u32[]{:S(2)}) copy-start(f32[1,1152]{1,0:T(1,128)} %stack.105) | copy-start | bytes 13828
  122.6 3.1 %copy-start.39 = (f32[1,1152]{1,0:T(1,128)S(1)}, f32[1,1152]{1,0:T(1,128)}, u32[]{:S(2)}) copy-start(f32[1,1152]{1,0:T(1,128)} %stack.99) | copy-start | bytes 13828
  122.6 3.1 %copy-start.40 = (f32[1,1152]{1,0:T(1,128)S(1)}, f32[1,1152]{1,0:T(1,128)}, u32[]{:S(2)}) copy-start(f32[1,1152]{1,0:T(1,128)} %stack.104) | copy-start | bytes 13828
  122.6 3.1 %copy-start.35 = (f32[1152]{0:T(1024)S(1)}, f32[1152]{0:T(1024)}, u32[]{:S(2)}) copy-start(f32[1152]{0:T(1024)} %get-tuple-element.13) | copy-start | bytes 13828
  122.6 3.1 %copy-start.34 = (f32[1152]{0:T(1024)S(1)}, f32[1152]{0:T(1024)}, u32[]{:S(2)}) copy-start(f32[1152]{0:T(1024)} %get-tuple-element.12) | copy-start | bytes 13828
  122.7 3.1 %copy-start.33 = (f32[1152]{0:T(1024)S(1)}, f32[1152]{0:T(1024)}, u32[]{:S(2)}) copy-start(f32[1152]{0:T(1024)} %get-tuple-element.14) | copy-start | bytes 13828
  (27 other events, 65.1 us)
Sparse Core Ops, SparseCore 0:
  126.7 134.8 all-reduce.18
where the time goes:
time: 272 us
  waiting for transfers between devices  150 us (55%)
  blocking collectives  62.4 us (23%)
  other arithmetic  23 us (8%)
  between operations  14.8 us (5%)
  local copies, waits for them, and re-layouts  11.6 us (4%)
  matrix products  5.35 us (2%)
  starting transfers between devices  5.18 us (2%)
    psum x1, waiting for transfers between devices, per_device(): lax.psum((point_local, depth_local, bias_local), ('dp', 'lon'))  127 us
    psum x1, blocking collectives, per_device(): lax.psum((point_local, depth_local, bias_local), ('dp', 'lon'))  62.4 us
    ppermute x4, waiting for transfers between devices, from_behind(): return lax.ppermute(block, axis, route)  23 us
  transfers between devices with their start and end apart: 5, of which 3 were waited for; matrix products, arithmetic and copies ran while one was open for 6% of the time, Pallas kernels for 0%

commit v1 on v0

--- a/solution.py
+++ b/solution.py
@@ -1,7 +1,15 @@
+import functools
+
 import jax
 import jax.numpy as jnp
 from jax import lax
+from jax.experimental import pallas as pl
+from jax.experimental.pallas import tpu as pltpu
 from jax.sharding import PartitionSpec as P
+
+MESH = pl.DeviceIdType.MESH
+F32 = jnp.float32
+BF16 = jnp.bfloat16
 
 RATE_A = 24
 RATE_B = 36
@@ -151,10 +159,416 @@
     return (feature_grad, depth_grad, point_grad, bias_grad)
 
 
+LANES = 128
+CHUNK = 160
+POINT_ROWS = 144
+FIRST = 80
+
+
+def ring(e, g):
+    return (g + e) % 3
+
+
+def widen(block):
+    wide = block.astype(F32)
+    return wide[0:24], wide[24:48]
+
+
+def join_rows(low, high):
+    return jnp.concatenate([low, high], axis=0)
+
+
+def fold(block):
+    total = block[0:8]
+    for at in range(8, block.shape[0], 8):
+        total = total + block[at : at + 8]
+    return total
+
+
+def edge_taps(wide):
+    rows = lax.broadcasted_iota(jnp.int32, (16, LANES), 0)
+    ahead = jnp.where(rows < 12, pltpu.roll(wide[32:48], 12, 0), 0.0)
+    behind = jnp.where(rows >= 4, pltpu.roll(wide[0:16], 4, 0), 0.0)
+    return ahead, behind
+
+
+def taps_a(dw_ref, lanes):
+    rows = [dw_ref[0, a, :, lanes].astype(F32) for a in range(3)]
+    return [[rows[a][e : e + 1] for e in range(3)] for a in range(3)]
+
+
+def taps_b(dw_ref, lanes):
+    rows = [dw_ref[1, a, :, lanes].astype(F32) for a in range(3)]
+    return [row[0:1] + row[1:2] + row[2:3] for row in rows]
+
+
+def lane_block(at):
+    return pl.ds(pl.multiple_of(at * LANES, LANES), LANES)
+
+
+def point_step(depth, weight, bias, upstream):
+    act = jnp.dot(depth, weight, preferred_element_type=F32) + bias
+    return (upstream.astype(F32) * gate_slope(act)).astype(BF16)
+
+
+def spread_back(pgrad_ref, pw_ref, branch, out_ref):
+    @pl.loop(0, 3)
+    def _(at):
+        cols = pl.ds(pl.multiple_of(at * 384, 384), 384)
+        out_ref[:, cols] = lax.dot_general(
+            pgrad_ref[...], pw_ref[branch, cols, :], (((1,), (1,)), ((), ())), preferred_element_type=F32
+        ).astype(BF16)
+
+
+def point_terms(depth_ref, pgrad_ref, wide_ref, acc, half):
+    @pl.loop(0, 3)
+    def _(at):
+        cols = pl.ds(pl.multiple_of(at * 384, 384), 384)
+        wide_ref[cols, :] = lax.dot_general(
+            depth_ref[:, cols], pgrad_ref[...], (((0,), (0,)), ((), ())), preferred_element_type=F32
+        )
+
+    @pl.loop(0, 4)
+    def _(at):
+        for upper in range(2):
+            for side in range(2):
+                start = pl.multiple_of((upper * 4 + at) * POINT_ROWS, 16)
+                block = wide_ref[pl.ds(start, POINT_ROWS), side * LANES : (side + 1) * LANES]
+                acc[half, side, upper, at, 0:POINT_ROWS, :] = block.astype(BF16)
+
+
+def small_slot(at):
+    return at // 8, (at // 4) % 2, at % 4
+
+
+def small_terms(taps_ref, pgrad_ref, acc, half):
+    for at in range(9):
+        y, x, z = small_slot(at)
+        block = taps_ref[:, at * LANES : (at + 1) * LANES]
+        acc[half, y, x, z, POINT_ROWS:CHUNK, :] = block.astype(BF16)
+    total = jnp.sum(pgrad_ref[...].astype(F32), axis=0, keepdims=True)
+    for at in range(2):
+        y, x, z = small_slot(9 + at)
+        block = jnp.broadcast_to(total[:, at * LANES : (at + 1) * LANES], (16, LANES))
+        acc[half, y, x, z, POINT_ROWS:CHUNK, :] = block.astype(BF16)
+    for at in range(11, 16):
+        y, x, z = small_slot(at)
+        acc[half, y, x, z, POINT_ROWS:CHUNK, :] = jnp.zeros((16, LANES), BF16)
+
+
+def whole_kernel(
+    images, feat_ref, dw_ref, pw_ref, bias_ref, cot_ref,
+    fgrad_ref, dgrad_out, pgrad_out, bgrad_out,
+    feat_in, cot_in, pg_in, depth_s, pg_a, pg_b, dg_a, dg_b, wide_s, taps_s,
+    acc, cur, fin, r0, r1y, r1x, r2y, r2x, r3, send_sem, recv_sem,
+):
+    dp = lax.axis_index("dp")
+    my = lax.axis_index("lon")
+    core = lax.rem(dp, 2)
+    mx = lax.rem(dp // 2, 2)
+    mz = dp // 4
+    other_y = {"dp": dp, "lon": 1 - my}
+    other_core = {"dp": dp + 1 - 2 * core, "lon": my}
+    other_x = {"dp": dp + 2 - 4 * mx, "lon": my}
+    other_z = [{"dp": lax.rem(dp + 4 * step, 16), "lon": my} for step in (1, 2, 3)]
+
+    barrier = pltpu.get_barrier_semaphore()
+    for peer in [other_y, other_core, other_x] + other_z:
+        pl.semaphore_signal(barrier, inc=1, device_id=peer, device_id_type=MESH)
+    pl.semaphore_wait(barrier, 6)
+
+    def send(at, src, dst, peer):
+        copy = pltpu.make_async_remote_copy(
+            src_ref=src, dst_ref=dst, send_sem=send_sem.at[at], recv_sem=recv_sem.at[at],
+            device_id=peer, device_id_type=MESH,
+        )
+        copy.start()
+        return copy
+
+    feat_copy = send(0, feat_ref.at[144:288], feat_in, other_y)
+    cot_copy = send(1, cot_ref.at[144:288, 0:256], cot_in, other_y)
+
+    @pl.loop(0, 9)
+    def _(at):
+        lanes = lane_block(at)
+        w = taps_b(dw_ref, lanes)
+        for col in range(9):
+            rows = pl.ds(col * 48, 48)
+            wide = feat_ref[rows, lanes].astype(F32)
+            ahead, behind = edge_taps(wide)
+            low = w[1] * wide[0:16] + w[2] * ahead
+            high = w[1] * wide[32:48] + w[0] * behind
+            depth = jnp.concatenate([low, w[1] * wide[16:32], high], axis=0)
+            depth_s[rows, lanes] = depth.astype(BF16)
+
+    pg_b[...] = point_step(depth_s[...], pw_ref[1], bias_ref[1:2, :], cot_ref[:, 256:512])
+    point_terms(depth_s, pg_b, wide_s, acc, 1)
+    spread_back(pg_b, pw_ref, 1, dg_b)
+
+    taps_s[...] = jnp.zeros_like(taps_s)
+
+    @pl.loop(0, 9)
+    def _(at):
+        lanes = lane_block(at)
+        sums = [jnp.zeros((8, LANES), F32) for _ in range(3)]
+        for col in range(9):
+            rows = pl.ds(col * 48, 48)
+            wide = feat_ref[rows, lanes].astype(F32)
+            grad = dg_b[rows, lanes].astype(F32)
+            ahead, behind = edge_taps(wide)
+            sums[0] = sums[0] + fold(behind * grad[32:48])
+            sums[1] = sums[1] + fold(wide * grad)
+            sums[2] = sums[2] + fold(ahead * grad[0:16])
+        for a in range(3):
+            total = jnp.sum(sums[a], axis=0, keepdims=True)
+            taps_s[3 * a : 3 * a + 3, lanes] = jnp.broadcast_to(total, (3, LANES))
+
+    small_terms(taps_s, pg_b, acc, 1)
+
+    feat_copy.wait()
+    cot_copy.wait()
+
+    def cell_rows(g, t):
+        return pl.ds((3 * g + t) * 48, 48)
+
+    def load_feat(g, t, lanes):
+        if g == 2:
+            return widen(feat_in[pl.ds(t * 48, 48), lanes])
+        return widen(feat_ref[pl.ds((6 * g + t) * 48, 48), lanes])
+
+    @pl.loop(0, 9)
+    def _(at):
+        lanes = lane_block(at)
+        w = taps_a(dw_ref, lanes)
+        for t in range(3):
+            cells = [load_feat(g, t, lanes) for g in range(3)]
+            for g in range(3):
+                low = high = 0.0
+                for e in (-1, 0, 1):
+                    src_low, src_high = cells[ring(e, g)]
+                    low = low + w[1][e + 1] * src_low + w[2][e + 1] * src_high
+                    high = high + w[1][e + 1] * src_high + w[0][e + 1] * src_low
+                depth_s[cell_rows(g, t), lanes] = join_rows(low, high).astype(BF16)
+
+    for g in range(3):
+        rows = pl.ds(144 * g, 144)
+        upstream = cot_in[...] if g == 2 else cot_ref[pl.ds(288 * g, 144), 0:256]
+        pg_a[rows, :] = point_step(depth_s[rows, :], pw_ref[0], bias_ref[0:1, :], upstream)
+    pg_copy = send(2, pg_a, pg_in, other_y)
+    point_terms(depth_s, pg_a, wide_s, acc, 0)
+    spread_back(pg_a, pw_ref, 0, dg_a)
+
+    @pl.loop(0, 9)
+    def _(at):
+        lanes = lane_block(at)
+        sums = [[jnp.zeros((8, LANES), F32) for _ in range(3)] for _ in range(3)]
+        for t in range(3):
+            cells = [load_feat(g, t, lanes) for g in range(3)]
+            for g in range(3):
+                grad_low, grad_high = widen(dg_a[cell_rows(g, t), lanes])
+                for e in (-1, 0, 1):
+                    src_low, src_high = cells[ring(e, g)]
+                    sums[0][e + 1] = sums[0][e + 1] + fold(src_low * grad_high)
+                    sums[1][e + 1] = sums[1][e + 1] + fold(src_low * grad_low + src_high * grad_high)
+                    sums[2][e + 1] = sums[2][e + 1] + fold(src_high * grad_low)
+        for a in range(3):
+            for e in range(3):
+                taps_s[3 * a + e : 3 * a + e + 1, lanes] = jnp.sum(sums[a][e], axis=0, keepdims=True)
+
+    small_terms(taps_s, pg_a, acc, 0)
+    sib_copy = send(3, acc.at[1 - core], r0, other_core)
+
+    def branch_b_grad(rows, lanes, w):
+        grad = dg_b[rows, lanes].astype(F32)
+        ahead, behind = edge_taps(grad)
+        low = w[1] * grad[0:16] + w[0] * ahead
+        high = w[1] * grad[32:48] + w[2] * behind
+        return jnp.concatenate([low, w[1] * grad[16:32], high], axis=0)
+
+    def branch_a_grad(w, grads, g):
+        low = high = 0.0
+        for e in (-1, 0, 1):
+            src_low, src_high = grads[ring(-e, g)]
+            low = low + w[1][e + 1] * src_low + w[0][e + 1] * src_high
+            high = high + w[1][e + 1] * src_high + w[2][e + 1] * src_low
+        return join_rows(low, high)
+
+    @pl.loop(0, 9)
+    def _(at):
+        lanes = lane_block(at)
+        w = taps_a(dw_ref, lanes)
+        wb = taps_b(dw_ref, lanes)
+        for t in range(3):
+            grads = [widen(dg_a[cell_rows(g, t), lanes]) for g in range(3)]
+            for g in range(2):
+                rows = pl.ds((6 * g + t) * 48, 48)
+                total = branch_a_grad(w, grads, g) + branch_b_grad(rows, lanes, wb)
+                fgrad_ref[rows, lanes] = total.astype(BF16)
+
+    sib_copy.wait()
+
+    @pl.loop(0, 4)
+    def _(z):
+        for y in range(2):
+            for x in range(2):
+                cur[y, x, z] = (acc[core, y, x, z].astype(F32) + r0[y, x, z].astype(F32)).astype(BF16)
+
+    rows_y = pl.ds(0, FIRST)
+    rows_x = pl.ds(FIRST, CHUNK - FIRST)
+    one_y = send(4, cur.at[1 - my, :, :, rows_y], r1y, other_y)
+    one_x = send(5, cur.at[:, 1 - mx, :, rows_x], r1x, other_x)
+
+    pg_copy.wait()
+    spread_back(pg_in, pw_ref, 0, dg_a)
+
+    @pl.loop(0, 9)
+    def _(at):
+        lanes = lane_block(at)
+        w = taps_a(dw_ref, lanes)
+        wb = taps_b(dw_ref, lanes)
+        for t in range(3):
+            grads = [widen(dg_a[cell_rows(g, t), lanes]) for g in range(3)]
+            rows = pl.ds((3 + t) * 48, 48)
+            total = branch_a_grad(w, grads, 2) + branch_b_grad(rows, lanes, wb)
+            fgrad_ref[rows, lanes] = total.astype(BF16)
+
+    one_y.wait()
+    one_x.wait()
+
+    def add_into(at, extra):
+        cur[at] = (cur[at].astype(F32) + extra.astype(F32)).astype(BF16)
+
+    @pl.loop(0, 4)
+    def _(z):
+        for k in range(2):
+            add_into((my, k, z, rows_y), r1y[k, z])
+            add_into((k, mx, z, rows_x), r1x[k, z])
+
+    two_x = send(6, cur.at[my, 1 - mx, :, rows_y], r2x, other_x)
+    two_y = send(7, cur.at[1 - my, mx, :, rows_x], r2y, other_y)
+    two_x.wait()
+    two_y.wait()
+
+    @pl.loop(0, 4)
+    def _(z):
+        add_into((my, mx, z, rows_y), r2x[z])
+        add_into((my, mx, z, rows_x), r2y[z])
+
+    three = [
+        send(8 + k, cur.at[my, mx, lax.rem(mz + k + 1, 4)], r3.at[k], other_z[k]) for k in range(3)
+    ]
+    for copy in three:
+        copy.wait()
+    total = cur[my, mx, mz].astype(F32)
+    for k in range(3):
+        total = total + r3[k].astype(F32)
+    fin[core, my, mx, mz] = (total * (1.0 / images)).astype(BF16)
+
+    def share(at, index, peer):
+        return send(at, fin.at[index], fin.at[index], peer)
+
+    for copy in [share(11 + k, (core, my, mx, mz), other_z[k]) for k in range(3)]:
+        copy.wait()
+    every = slice(None)
+    five = [
+        share(14, (core, my, mx, every, rows_y), other_x),
+        share(15, (core, my, mx, every, rows_x), other_y),
+    ]
+    for copy in five:
+        copy.wait()
+    six = [
+        share(16, (core, my, every, every, rows_y), other_y),
+        share(17, (core, every, mx, every, rows_x), other_x),
+    ]
+    for copy in six:
+        copy.wait()
+    share(18, (core,), other_core).wait()
+
+    for half in range(2):
+        @pl.loop(0, 4)
+        def _(at):
+            for upper in range(2):
+                for side in range(2):
+                    start = pl.multiple_of((upper * 4 + at) * POINT_ROWS, 16)
+                    block = fin[half, side, upper, at, 0:POINT_ROWS, :]
+                    pgrad_out[half, pl.ds(start, POINT_ROWS), side * LANES : (side + 1) * LANES] = block
+
+        for at in range(9):
+            y, x, z = small_slot(at)
+            block = fin[half, y, x, z, POINT_ROWS:CHUNK, :].astype(F32)
+            for a in range(3):
+                part = block[3 * a : 3 * a + 3].astype(BF16)
+                dgrad_out[half, a, :, at * LANES : (at + 1) * LANES] = part
+        for at in range(2):
+            y, x, z = small_slot(9 + at)
+            block = fin[half, y, x, z, POINT_ROWS:CHUNK, :].astype(F32)
+            bgrad_out[half : half + 1, at * LANES : (at + 1) * LANES] = block[0:1]
+
+
+def fused_step(features, depth_w, point_w, point_bias, cotangent):
+    images = lax.axis_size("dp") * features.shape[0]
+    cells, channels, outputs = 432, features.shape[3], point_w.shape[2]
+    scratch = [
+        pltpu.VMEM((144, channels), BF16),
+        pltpu.VMEM((144, outputs), BF16),
+        pltpu.VMEM((cells, outputs), BF16),
+        pltpu.VMEM((cells, channels), BF16),
+        pltpu.VMEM((cells, outputs), BF16),
+        pltpu.VMEM((cells, outputs), BF16),
+        pltpu.VMEM((cells, channels), BF16),
+        pltpu.VMEM((cells, channels), BF16),
+        pltpu.VMEM((channels, outputs), F32),
+        pltpu.VMEM((16, channels), F32),
+        pltpu.VMEM((2, 2, 2, 4, CHUNK, LANES), BF16),
+        pltpu.VMEM((2, 2, 4, CHUNK, LANES), BF16),
+        pltpu.VMEM((2, 2, 2, 4, CHUNK, LANES), BF16),
+        pltpu.VMEM((2, 2, 4, CHUNK, LANES), BF16),
+        pltpu.VMEM((2, 4, FIRST, LANES), BF16),
+        pltpu.VMEM((2, 4, FIRST, LANES), BF16),
+        pltpu.VMEM((4, FIRST, LANES), BF16),
+        pltpu.VMEM((4, FIRST, LANES), BF16),
+        pltpu.VMEM((3, CHUNK, LANES), BF16),
+        pltpu.SemaphoreType.DMA((19,)),
+        pltpu.SemaphoreType.DMA((19,)),
+    ]
+    in_vmem = pl.BlockSpec(memory_space=pltpu.VMEM)
+    feature_grad, depth_grad, point_grad, bias_grad = pl.pallas_call(
+        functools.partial(whole_kernel, images),
+        out_shape=(
+            jax.ShapeDtypeStruct((cells, channels), BF16),
+            jax.ShapeDtypeStruct(depth_w.shape, BF16),
+            jax.ShapeDtypeStruct(point_w.shape, BF16),
+            jax.ShapeDtypeStruct(point_bias.shape, F32),
+        ),
+        in_specs=[in_vmem] * 5,
+        out_specs=[in_vmem] * 4,
+        scratch_shapes=scratch,
+        compiler_params=pltpu.CompilerParams(
+            collective_id=0, has_side_effects=True, vmem_limit_bytes=40 * 1024 * 1024
+        ),
+        cost_estimate=pl.CostEstimate(flops=2 * 7 * cells * channels * outputs, bytes_accessed=8000000, transcendentals=0),
+    )(features.reshape(cells, channels), depth_w, point_w, point_bias, cotangent.reshape(cells, 2 * outputs))
+    return feature_grad.reshape(features.shape), depth_grad, point_grad, bias_grad
+
+
+def fits_fused(mesh):
+    return dict(mesh.shape) == {"dp": 16, "lon": 2}
+
+
+def chosen_step(mesh):
+    def step(features, depth_w, point_w, point_bias, cotangent):
+        arguments = (features, depth_w, point_w, point_bias, cotangent)
+        if fits_fused(mesh) and features.shape == (1, 9, 48, 1152) and point_w.shape[2] == 256:
+            return fused_step(*arguments)
+        return per_device(*arguments)
+
+    return step
+
+
 def solution(mesh):
     placed = (P("dp", "lon", None, None), P(), P(), P(), P("dp", "lon", None, None))
     return jax.shard_map(
-        per_device,
+        chosen_step(mesh),
         mesh=mesh,
         in_specs=placed,
         out_specs=(P("dp", "lon", None, None), P(), P(), P()),

time: 272 us -> 60.6 us (0.22)
  waiting for transfers between devices: 150 us -> 0 us
  blocking collectives: 62.4 us -> 0 us
  Pallas kernels: 0 us -> 51.5 us
  other arithmetic: 23 us -> 0 us
  between operations: 14.8 us -> 0.65 us
  matrix products: 5.35 us -> 0 us
  starting transfers between devices: 5.18 us -> 0 us
  local copies, waits for them, and re-layouts: 11.6 us -> 8.16 us
    psum x1 -> x0, waiting for transfers between devices: 127 us -> none  [per_device(): lax.psum((point_local, depth_local, bias_local), ('dp', 'lon'))]
    psum x1 -> x0, blocking collectives: 62.4 us -> none  [per_device(): lax.psum((point_local, depth_local, bias_local), ('dp', 'lon'))]
    pallas_call x0 -> x1, Pallas kernels: none -> 51.5 us  [fused_step(): pl.pallas_call(functools.partial(whole_kernel, images), out_shape=(jax.Sh...]
    ppermute x4 -> x0, waiting for transfers between devices: 23 us -> none  [from_behind(): return lax.ppermute(block, axis, route)]
    convert_element_type x7 -> x0, other arithmetic: 11.6 us -> none  [the longest x1 4.94 us: per_device(): feature_grad = grad_field.astype(jnp.bfloat16)]
    unnamed x93 -> x13, local copies, waits for them, and re-layouts: 1.44 us -> 8.16 us
    another operation x12 -> x0, local copies, waits for them, and re-layouts: 5.38 us -> none  [the longest x9 5.36 us: per_device(): tap_rows.append(jnp.stack(tap_cols))]
    dot_general x6 -> x0, matrix products: 5.35 us -> none  [the longest x2 3.1 us: per_device(): lax.dot_general(flat_depth, pgrad, (((0,), (0,)), ((), ())), preferred_el...]
  transfers between devices with their start and end apart: 5 -> 0, of which waited for: 3 -> 0; matrix products, arithmetic and copies ran while one was open for 6% -> 0% of each run, Pallas kernels for 0% -> 0%
where the time goes in v1:
time: 60.6 us; the launch traced here: 60.3 us
  Pallas kernels  51.5 us (85%)
  local copies, waits for them, and re-layouts  8.16 us (13%)
  between operations  0.65 us (1%)
    pallas_call x1, Pallas kernels, fused_step(): pl.pallas_call(functools.partial(whole_kernel, images), out_shape=(jax.Sh...  51.5 us
    unnamed x13, local copies, waits for them, and re-layouts  8.16 us

profile of v1, /device:TPU:0, one launch (start us, length us, event | category | flops | bytes accessed | tf_op | source)
XLA Modules:
  0.0 60.3 jit_solution(11596472282086994819)
XLA Ops:
  0.6 0.8 %copy.9.dw_ref = bf16[2,3,3,1152]{3,2,1,0:T(4,128)(2,1)S(1)} copy(bf16[2,3,3,1152]{3,0,2,1:T(2,128)(2,1)} %param.6) | data formatting | bytes 82944 | tf_op args[1]
  1.4 0.0 copy-start
  1.5 1.3 %copy-done = bf16[2,1152,256]{2,1,0:T(8,128)(2,1)S(1)} copy-done((bf16[2,1152,256]{2,1,0:T(8,128)(2,1)S(1)}, bf16[2,1152,256]{2,1,0:T(8,128)(2,1)}, u32[]{:S(2)}) %copy-start) | copy-done | bytes 1179672
  2.7 0.0 copy-start.1
  2.7 1.2 %copy-done.1 = bf16[1,9,48,1152]{3,2,1,0:T(8,128)(2,1)S(1)} copy-done((bf16[1,9,48,1152]{3,2,1,0:T(8,128)(2,1)S(1)}, bf16[1,9,48,1152]{3,2,1,0:T(8,128)(2,1)}, u32[]{:S(2)}) %copy-start.1) | copy-done | bytes 995352
  3.9 0.0 copy-start.2
  3.9 1.0 %copy-done.2 = bf16[1,9,48,512]{3,2,1,0:T(8,128)(2,1)S(1)} copy-done((bf16[1,9,48,512]{3,2,1,0:T(8,128)(2,1)S(1)}, bf16[1,9,48,512]{3,2,1,0:T(8,128)(2,1)}, u32[]{:S(2)}) %copy-start.2) | copy-done | bytes 442392
  4.9 0.0 copy-start.3
  4.9 0.7 %copy-done.3 = f32[2,256]{1,0:T(2,128)S(1)} copy-done((f32[2,256]{1,0:T(2,128)S(1)}, f32[2,256]{1,0:T(2,128)}, u32[]{:S(2)}) %copy-start.3) | copy-done | bytes 2072
  5.6 51.5 %shard_map.84 = (bf16[432,1152]{1,0:T(8,128)(2,1)S(1)}, bf16[2,3,3,1152]{3,2,1,0:T(4,128)(2,1)S(1)}, bf16[2,1152,256]{2,1,0:T(8,128)(2,1)S(1)}, f32[2,256]{1,0:T(2,128)S(1)}) custom-call(bf16[432,1152]{1,0:T(8,128)(2,1)S(1)} %bitcast.4, bf16[2,3,3,1152]{3,2,1,0:T(4,128)(2,1)S(1)} %copy.9.dw_ref, bf16[2,1152,256]{2,1,0:T(8,128)(2,1)S(1)} %copy-done, ...), custom_call_target="tpu_custom_call" | custom-call | flops 1783627776 | bytes 8000000 | tf_op jit(solution)/shard_map/pallas_call | solution.py:535
  57.1 0.7 %copy.10 = bf16[2,3,3,1152]{3,0,2,1:T(2,128)(2,1)} copy(bf16[2,3,3,1152]{3,2,1,0:T(4,128)(2,1)S(1)} %get-tuple-element.13) | data formatting | bytes 82944
  57.8 0.9 %copy.14 = bf16[1,9,48,1152]{3,2,1,0:T(8,128)(2,1)} copy(bf16[1,9,48,1152]{3,2,1,0:T(8,128)(2,1)S(1)} %bitcast.3) | data formatting | bytes 1990656
  58.7 1.0 %copy.15 = bf16[2,1152,256]{2,1,0:T(8,128)(2,1)} copy(bf16[2,1152,256]{2,1,0:T(8,128)(2,1)S(1)} %get-tuple-element.22) | data formatting | bytes 2359296
  59.7 0.6 copy.16
Async XLA Ops:
  1.4 1.3 %copy-start = (bf16[2,1152,256]{2,1,0:T(8,128)(2,1)S(1)}, bf16[2,1152,256]{2,1,0:T(8,128)(2,1)}, u32[]{:S(2)}) copy-start(bf16[2,1152,256]{2,1,0:T(8,128)(2,1)} %pw_ref.1) | copy-start | bytes 3538948
  2.7 1.2 %copy-start.1 = (bf16[1,9,48,1152]{3,2,1,0:T(8,128)(2,1)S(1)}, bf16[1,9,48,1152]{3,2,1,0:T(8,128)(2,1)}, u32[]{:S(2)}) copy-start(bf16[1,9,48,1152]{3,2,1,0:T(8,128)(2,1)} %param.5) | copy-start | bytes 2985988
  3.9 1.0 %copy-start.2 = (bf16[1,9,48,512]{3,2,1,0:T(8,128)(2,1)S(1)}, bf16[1,9,48,512]{3,2,1,0:T(8,128)(2,1)}, u32[]{:S(2)}) copy-start(bf16[1,9,48,512]{3,2,1,0:T(8,128)(2,1)} %param.9) | copy-start | bytes 1327108
  4.9 0.7 %copy-start.3 = (f32[2,256]{1,0:T(2,128)S(1)}, f32[2,256]{1,0:T(2,128)}, u32[]{:S(2)}) copy-start(f32[2,256]{1,0:T(2,128)} %bias_ref.1) | copy-start | bytes 6148

commit v2 on v1

--- a/solution.py
+++ b/solution.py
@@ -160,9 +160,10 @@
 
 
 LANES = 128
-CHUNK = 160
-POINT_ROWS = 144
-FIRST = 80
+CHUNK = 80
+POINT_ROWS = 72
+BULK = 64
+SENDS = 33
 
 
 def ring(e, g):
@@ -192,14 +193,17 @@
     return ahead, behind
 
 
+def tap_row(dw_ref, branch, a, e, lanes):
+    return dw_ref[a, e, :, lanes].astype(F32)[branch : branch + 1]
+
+
 def taps_a(dw_ref, lanes):
-    rows = [dw_ref[0, a, :, lanes].astype(F32) for a in range(3)]
-    return [[rows[a][e : e + 1] for e in range(3)] for a in range(3)]
+    return [[tap_row(dw_ref, 0, a, e, lanes) for e in range(3)] for a in range(3)]
 
 
 def taps_b(dw_ref, lanes):
-    rows = [dw_ref[1, a, :, lanes].astype(F32) for a in range(3)]
-    return [row[0:1] + row[1:2] + row[2:3] for row in rows]
+    rows = [[tap_row(dw_ref, 1, a, e, lanes) for e in range(3)] for a in range(3)]
+    return [row[0] + row[1] + row[2] for row in rows]
 
 
 def lane_block(at):
@@ -220,7 +224,11 @@
         ).astype(BF16)
 
 
-def point_terms(depth_ref, pgrad_ref, wide_ref, acc, half):
+def place(at):
+    return at // 8, lax.rem(at // 4, 2), lax.rem(at, 4)
+
+
+def point_terms(depth_ref, pgrad_ref, wide_ref, acc, branch):
     @pl.loop(0, 3)
     def _(at):
         cols = pl.ds(pl.multiple_of(at * 384, 384), 384)
@@ -228,39 +236,64 @@
             depth_ref[:, cols], pgrad_ref[...], (((0,), (0,)), ((), ())), preferred_element_type=F32
         )
 
-    @pl.loop(0, 4)
-    def _(at):
-        for upper in range(2):
-            for side in range(2):
-                start = pl.multiple_of((upper * 4 + at) * POINT_ROWS, 16)
-                block = wide_ref[pl.ds(start, POINT_ROWS), side * LANES : (side + 1) * LANES]
-                acc[half, side, upper, at, 0:POINT_ROWS, :] = block.astype(BF16)
-
-
-def small_slot(at):
-    return at // 8, (at // 4) % 2, at % 4
-
-
-def small_terms(taps_ref, pgrad_ref, acc, half):
-    for at in range(9):
-        y, x, z = small_slot(at)
-        block = taps_ref[:, at * LANES : (at + 1) * LANES]
-        acc[half, y, x, z, POINT_ROWS:CHUNK, :] = block.astype(BF16)
+    @pl.loop(0, 16)
+    def _(at):
+        y, x, z = place(at)
+        rows = pl.ds(pl.multiple_of(at * POINT_ROWS, 8), BULK)
+        for side in range(2):
+            block = wide_ref[rows, side * LANES : (side + 1) * LANES]
+            acc[branch, side, y, x, z, 0:BULK, :] = block.astype(BF16)
+
+
+def small_terms(wide_ref, taps_ref, pgrad_ref, acc, branch):
     total = jnp.sum(pgrad_ref[...].astype(F32), axis=0, keepdims=True)
     for at in range(2):
-        y, x, z = small_slot(9 + at)
-        block = jnp.broadcast_to(total[:, at * LANES : (at + 1) * LANES], (16, LANES))
-        acc[half, y, x, z, POINT_ROWS:CHUNK, :] = block.astype(BF16)
-    for at in range(11, 16):
-        y, x, z = small_slot(at)
-        acc[half, y, x, z, POINT_ROWS:CHUNK, :] = jnp.zeros((16, LANES), BF16)
+        taps_ref[1, 9 + at, 0:1, :] = total[:, at * LANES : (at + 1) * LANES]
+
+    @pl.loop(0, 16)
+    def _(at):
+        y, x, z = place(at)
+        rows = pl.ds(pl.multiple_of(at * POINT_ROWS + BULK, 8), POINT_ROWS - BULK)
+        for side in range(2):
+            block = wide_ref[rows, side * LANES : (side + 1) * LANES]
+            block = jnp.concatenate([block, taps_ref[side, at]], axis=0)
+            acc[branch, side, y, x, z, BULK:CHUNK, :] = block.astype(BF16)
+
+
+def store_results(fin, branch, pgrad_out, bgrad_out):
+    @pl.loop(0, 8)
+    def _(pair):
+        y, x, z = place(pair * 2)
+        rows = pl.ds(pl.multiple_of(pair * 2 * POINT_ROWS, 16), 2 * POINT_ROWS)
+        for side in range(2):
+            blocks = [fin[branch, side, y, x, z + k].astype(F32)[0:POINT_ROWS] for k in range(2)]
+            pgrad_out[branch, rows, side * LANES : (side + 1) * LANES] = jnp.concatenate(blocks, axis=0).astype(BF16)
+
+    for at in range(2):
+        block = fin[branch, 1, 1, 0, 1 + at, BULK:CHUNK, :].astype(F32)
+        bgrad_out[branch : branch + 1, at * LANES : (at + 1) * LANES] = block[8:9]
+
+
+def store_taps(fin, dgrad_out):
+    for at in range(9):
+        lanes = slice(at * LANES, (at + 1) * LANES)
+        y, x, z = at // 8, (at // 4) % 2, at % 4
+        blocks = [
+            [fin[branch, side, y, x, z, BULK:CHUNK, :].astype(F32)[8:16] for side in range(2)] for branch in range(2)
+        ]
+        for tap in range(9):
+            side, row = tap // 8, tap % 8
+            pair = [blocks[branch][side][row : row + 1] for branch in range(2)]
+            dgrad_out[tap // 3, tap % 3, :, lanes] = jnp.concatenate(pair, axis=0).astype(BF16)
 
 
 def whole_kernel(
-    images, feat_ref, dw_ref, pw_ref, bias_ref, cot_ref,
+    images, feat_hbm, dw_hbm, pw_hbm, bias_hbm, cot_hbm,
+    fgrad_hbm, dgrad_hbm, pgrad_hbm, bgrad_hbm,
     fgrad_ref, dgrad_out, pgrad_out, bgrad_out,
+    feat_ref, dw_ref, pw_ref, bias_ref, cot_ref,
     feat_in, cot_in, pg_in, depth_s, pg_a, pg_b, dg_a, dg_b, wide_s, taps_s,
-    acc, cur, fin, r0, r1y, r1x, r2y, r2x, r3, send_sem, recv_sem,
+    acc, cur, fin, r0, bx, bz, by, a1y, a1x, a2x, a2y, a3, load_sem, store_sem, send_sem, recv_sem,
 ):
     dp = lax.axis_index("dp")
     my = lax.axis_index("lon")
@@ -272,12 +305,24 @@
     other_x = {"dp": dp + 2 - 4 * mx, "lon": my}
     other_z = [{"dp": lax.rem(dp + 4 * step, 16), "lon": my} for step in (1, 2, 3)]
 
+    loads = [
+        pltpu.make_async_copy(src, dst, load_sem.at[at])
+        for at, (src, dst) in enumerate(
+            [(feat_hbm, feat_ref), (dw_hbm, dw_ref), (pw_hbm, pw_ref), (bias_hbm, bias_ref), (cot_hbm, cot_ref)]
+        )
+    ]
+    for copy in loads:
+        copy.start()
+
     barrier = pltpu.get_barrier_semaphore()
     for peer in [other_y, other_core, other_x] + other_z:
         pl.semaphore_signal(barrier, inc=1, device_id=peer, device_id_type=MESH)
     pl.semaphore_wait(barrier, 6)
 
-    def send(at, src, dst, peer):
+    numbers = iter(range(SENDS))
+
+    def send(src, dst, peer):
+        at = next(numbers)
         copy = pltpu.make_async_remote_copy(
             src_ref=src, dst_ref=dst, send_sem=send_sem.at[at], recv_sem=recv_sem.at[at],
             device_id=peer, device_id_type=MESH,
@@ -285,8 +330,47 @@
         copy.start()
         return copy
 
-    feat_copy = send(0, feat_ref.at[144:288], feat_in, other_y)
-    cot_copy = send(1, cot_ref.at[144:288, 0:256], cot_in, other_y)
+    stores = []
+
+    def store(src, dst):
+        copy = pltpu.make_async_copy(src, dst, store_sem.at[len(stores)])
+        copy.start()
+        stores.append(copy)
+
+    def finish(copies):
+        for copy in copies:
+            copy.wait()
+
+    feat_copy = send(feat_hbm.at[144:288], feat_in, other_y)
+    cot_copy = send(cot_hbm.at[144:288, 0:256], cot_in, other_y)
+    finish(loads)
+    taps_s[...] = jnp.zeros_like(taps_s)
+
+    def add_into(at, extra):
+        cur[at] = (cur[at].astype(F32) + extra.astype(F32)).astype(BF16)
+
+    def share(index, peer):
+        return send(fin.at[index], fin.at[index], peer)
+
+    def send_half(branch, rows):
+        return send(acc.at[branch, 1 - core, :, :, :, rows], r0.at[branch, :, :, :, rows], other_core)
+
+    def add_halves(branch):
+        @pl.loop(0, 4)
+        def _(z):
+            for y in range(2):
+                for x in range(2):
+                    total = acc[branch, core, y, x, z].astype(F32) + r0[branch, y, x, z].astype(F32)
+                    cur[branch, y, x, z] = total.astype(BF16)
+
+    def settle(branch, extras):
+        total = cur[branch, my, mx, mz].astype(F32)
+        for extra in extras:
+            total = total + extra.astype(F32)
+        fin[branch, core, my, mx, mz] = (total * (1.0 / images)).astype(BF16)
+
+    every = slice(None)
+    lower, upper = pl.ds(0, 2), pl.ds(2, 2)
 
     @pl.loop(0, 9)
     def _(at):
@@ -303,9 +387,8 @@
 
     pg_b[...] = point_step(depth_s[...], pw_ref[1], bias_ref[1:2, :], cot_ref[:, 256:512])
     point_terms(depth_s, pg_b, wide_s, acc, 1)
+    b_step = [send_half(1, pl.ds(0, BULK))]
     spread_back(pg_b, pw_ref, 1, dg_b)
-
-    taps_s[...] = jnp.zeros_like(taps_s)
 
     @pl.loop(0, 9)
     def _(at):
@@ -321,9 +404,15 @@
             sums[2] = sums[2] + fold(ahead * grad[0:16])
         for a in range(3):
             total = jnp.sum(sums[a], axis=0, keepdims=True)
-            taps_s[3 * a : 3 * a + 3, lanes] = jnp.broadcast_to(total, (3, LANES))
-
-    small_terms(taps_s, pg_b, acc, 1)
+            for e in range(3):
+                tap = 3 * a + e
+                taps_s[tap // 8, at, tap % 8 : tap % 8 + 1, :] = total
+
+    small_terms(wide_s, taps_s, pg_b, acc, 1)
+    b_step.append(send_half(1, pl.ds(BULK, CHUNK - BULK)))
+    finish(b_step)
+    add_halves(1)
+    b_step = [send(cur.at[1, :, 1 - mx], bx, other_x)]
 
     feat_copy.wait()
     cot_copy.wait()
@@ -354,8 +443,19 @@
         rows = pl.ds(144 * g, 144)
         upstream = cot_in[...] if g == 2 else cot_ref[pl.ds(288 * g, 144), 0:256]
         pg_a[rows, :] = point_step(depth_s[rows, :], pw_ref[0], bias_ref[0:1, :], upstream)
-    pg_copy = send(2, pg_a, pg_in, other_y)
+    pg_copy = send(pg_a, pg_in, other_y)
+
+    finish(b_step)
+
+    @pl.loop(0, 4)
+    def _(z):
+        for y in range(2):
+            add_into((1, y, mx, z), bx[y, z])
+
+    b_step = [send(cur.at[1, :, mx, lax.rem(mz + k + 1, 4)], bz.at[k], other_z[k]) for k in range(3)]
+
     point_terms(depth_s, pg_a, wide_s, acc, 0)
+    a_step = [send_half(0, pl.ds(0, BULK))]
     spread_back(pg_a, pw_ref, 0, dg_a)
 
     @pl.loop(0, 9)
@@ -373,10 +473,30 @@
                     sums[2][e + 1] = sums[2][e + 1] + fold(src_high * grad_low)
         for a in range(3):
             for e in range(3):
-                taps_s[3 * a + e : 3 * a + e + 1, lanes] = jnp.sum(sums[a][e], axis=0, keepdims=True)
-
-    small_terms(taps_s, pg_a, acc, 0)
-    sib_copy = send(3, acc.at[1 - core], r0, other_core)
+                tap = 3 * a + e
+                taps_s[tap // 8, at, tap % 8 : tap % 8 + 1, :] = jnp.sum(sums[a][e], axis=0, keepdims=True)
+
+    small_terms(wide_s, taps_s, pg_a, acc, 0)
+    a_step.append(send_half(0, pl.ds(BULK, CHUNK - BULK)))
+
+    finish(b_step)
+    for y in range(2):
+        total = cur[1, y, mx, mz].astype(F32)
+        for k in range(3):
+            total = total + bz[k, y].astype(F32)
+        cur[1, y, mx, mz] = total.astype(BF16)
+    b_step = [send(cur.at[1, 1 - my, mx, mz], by, other_y)]
+
+    finish(a_step)
+    add_halves(0)
+    a_step = [
+        send(cur.at[0, 1 - my, :, lower], a1y, other_y),
+        send(cur.at[0, :, 1 - mx, upper], a1x, other_x),
+    ]
+
+    finish(b_step)
+    settle(1, [by[...]])
+    b_step = [share((1, core, my, mx, mz), other_y)]
 
     def branch_b_grad(rows, lanes, w):
         grad = dg_b[rows, lanes].astype(F32)
@@ -405,18 +525,18 @@
                 total = branch_a_grad(w, grads, g) + branch_b_grad(rows, lanes, wb)
                 fgrad_ref[rows, lanes] = total.astype(BF16)
 
-    sib_copy.wait()
-
-    @pl.loop(0, 4)
-    def _(z):
-        for y in range(2):
-            for x in range(2):
-                cur[y, x, z] = (acc[core, y, x, z].astype(F32) + r0[y, x, z].astype(F32)).astype(BF16)
-
-    rows_y = pl.ds(0, FIRST)
-    rows_x = pl.ds(FIRST, CHUNK - FIRST)
-    one_y = send(4, cur.at[1 - my, :, :, rows_y], r1y, other_y)
-    one_x = send(5, cur.at[:, 1 - mx, :, rows_x], r1x, other_x)
+    finish(b_step)
+    b_step = [share((1, core, every, mx, mz), peer) for peer in other_z]
+
+    finish(a_step)
+    for k in range(2):
+        for z in range(2):
+            add_into((0, my, k, z), a1y[k, z])
+            add_into((0, k, mx, 2 + z), a1x[k, z])
+    a_step = [
+        send(cur.at[0, my, 1 - mx, lower], a2x, other_x),
+        send(cur.at[0, 1 - my, mx, upper], a2y, other_y),
+    ]
 
     pg_copy.wait()
     spread_back(pg_in, pw_ref, 0, dg_a)
@@ -432,83 +552,63 @@
             total = branch_a_grad(w, grads, 2) + branch_b_grad(rows, lanes, wb)
             fgrad_ref[rows, lanes] = total.astype(BF16)
 
-    one_y.wait()
-    one_x.wait()
-
-    def add_into(at, extra):
-        cur[at] = (cur[at].astype(F32) + extra.astype(F32)).astype(BF16)
-
-    @pl.loop(0, 4)
-    def _(z):
-        for k in range(2):
-            add_into((my, k, z, rows_y), r1y[k, z])
-            add_into((k, mx, z, rows_x), r1x[k, z])
-
-    two_x = send(6, cur.at[my, 1 - mx, :, rows_y], r2x, other_x)
-    two_y = send(7, cur.at[1 - my, mx, :, rows_x], r2y, other_y)
-    two_x.wait()
-    two_y.wait()
-
-    @pl.loop(0, 4)
-    def _(z):
-        add_into((my, mx, z, rows_y), r2x[z])
-        add_into((my, mx, z, rows_x), r2y[z])
-
-    three = [
-        send(8 + k, cur.at[my, mx, lax.rem(mz + k + 1, 4)], r3.at[k], other_z[k]) for k in range(3)
+    store(fgrad_ref, fgrad_hbm)
+
+    finish(a_step)
+    for z in range(2):
+        add_into((0, my, mx, z), a2x[z])
+        add_into((0, my, mx, 2 + z), a2y[z])
+    a_step = [send(cur.at[0, my, mx, lax.rem(mz + k + 1, 4)], a3.at[k], other_z[k]) for k in range(3)]
+
+    finish(b_step)
+    b_step = [share((1, core, every, mx), other_x)]
+
+    finish(a_step)
+    settle(0, [a3[k] for k in range(3)])
+    a_step = [share((0, core, my, mx, mz), peer) for peer in other_z]
+
+    finish(b_step)
+    b_step = [share((1, core), other_core)]
+
+    finish(a_step)
+    a_step = [
+        share((0, core, my, mx, lower), other_x),
+        share((0, core, my, mx, upper), other_y),
     ]
-    for copy in three:
-        copy.wait()
-    total = cur[my, mx, mz].astype(F32)
-    for k in range(3):
-        total = total + r3[k].astype(F32)
-    fin[core, my, mx, mz] = (total * (1.0 / images)).astype(BF16)
-
-    def share(at, index, peer):
-        return send(at, fin.at[index], fin.at[index], peer)
-
-    for copy in [share(11 + k, (core, my, mx, mz), other_z[k]) for k in range(3)]:
-        copy.wait()
-    every = slice(None)
-    five = [
-        share(14, (core, my, mx, every, rows_y), other_x),
-        share(15, (core, my, mx, every, rows_x), other_y),
+
+    finish(b_step)
+    store_results(fin, 1, pgrad_out, bgrad_out)
+    store(pgrad_out.at[1], pgrad_hbm.at[1])
+
+    finish(a_step)
+    a_step = [
+        share((0, core, my, every, lower), other_y),
+        share((0, core, every, mx, upper), other_x),
     ]
-    for copy in five:
-        copy.wait()
-    six = [
-        share(16, (core, my, every, every, rows_y), other_y),
-        share(17, (core, every, mx, every, rows_x), other_x),
-    ]
-    for copy in six:
-        copy.wait()
-    share(18, (core,), other_core).wait()
-
-    for half in range(2):
-        @pl.loop(0, 4)
-        def _(at):
-            for upper in range(2):
-                for side in range(2):
-                    start = pl.multiple_of((upper * 4 + at) * POINT_ROWS, 16)
-                    block = fin[half, side, upper, at, 0:POINT_ROWS, :]
-                    pgrad_out[half, pl.ds(start, POINT_ROWS), side * LANES : (side + 1) * LANES] = block
-
-        for at in range(9):
-            y, x, z = small_slot(at)
-            block = fin[half, y, x, z, POINT_ROWS:CHUNK, :].astype(F32)
-            for a in range(3):
-                part = block[3 * a : 3 * a + 3].astype(BF16)
-                dgrad_out[half, a, :, at * LANES : (at + 1) * LANES] = part
-        for at in range(2):
-            y, x, z = small_slot(9 + at)
-            block = fin[half, y, x, z, POINT_ROWS:CHUNK, :].astype(F32)
-            bgrad_out[half : half + 1, at * LANES : (at + 1) * LANES] = block[0:1]
+    finish(a_step)
+    finish([share((0, core), other_core)])
+    store_results(fin, 0, pgrad_out, bgrad_out)
+    store(pgrad_out.at[0], pgrad_hbm.at[0])
+    store(bgrad_out, bgrad_hbm)
+    store_taps(fin, dgrad_out)
+    store(dgrad_out, dgrad_hbm)
+    finish(stores)
 
 
 def fused_step(features, depth_w, point_w, point_bias, cotangent):
     images = lax.axis_size("dp") * features.shape[0]
     cells, channels, outputs = 432, features.shape[3], point_w.shape[2]
+    chunk = (CHUNK, LANES)
     scratch = [
+        pltpu.VMEM((cells, channels), BF16),
+        pltpu.VMEM((3, 3, 2, channels), BF16),
+        pltpu.VMEM((2, channels, outputs), BF16),
+        pltpu.VMEM((2, outputs), F32),
+        pltpu.VMEM((cells, channels), BF16),
+        pltpu.VMEM((3, 3, 2, channels), BF16),
+        pltpu.VMEM((2, channels, outputs), BF16),
+        pltpu.VMEM((2, outputs), F32),
+        pltpu.VMEM((cells, 2 * outputs), BF16),
         pltpu.VMEM((144, channels), BF16),
         pltpu.VMEM((144, outputs), BF16),
         pltpu.VMEM((cells, outputs), BF16),
@@ -518,37 +618,42 @@
         pltpu.VMEM((cells, channels), BF16),
         pltpu.VMEM((cells, channels), BF16),
         pltpu.VMEM((channels, outputs), F32),
-        pltpu.VMEM((16, channels), F32),
-        pltpu.VMEM((2, 2, 2, 4, CHUNK, LANES), BF16),
-        pltpu.VMEM((2, 2, 4, CHUNK, LANES), BF16),
-        pltpu.VMEM((2, 2, 2, 4, CHUNK, LANES), BF16),
-        pltpu.VMEM((2, 2, 4, CHUNK, LANES), BF16),
-        pltpu.VMEM((2, 4, FIRST, LANES), BF16),
-        pltpu.VMEM((2, 4, FIRST, LANES), BF16),
-        pltpu.VMEM((4, FIRST, LANES), BF16),
-        pltpu.VMEM((4, FIRST, LANES), BF16),
-        pltpu.VMEM((3, CHUNK, LANES), BF16),
-        pltpu.SemaphoreType.DMA((19,)),
-        pltpu.SemaphoreType.DMA((19,)),
+        pltpu.VMEM((2, 16, 8, LANES), F32),
+        pltpu.VMEM((2, 2, 2, 2, 4) + chunk, BF16),
+        pltpu.VMEM((2, 2, 2, 4) + chunk, BF16),
+        pltpu.VMEM((2, 2, 2, 2, 4) + chunk, BF16),
+        pltpu.VMEM((2, 2, 2, 4) + chunk, BF16),
+        pltpu.VMEM((2, 4) + chunk, BF16),
+        pltpu.VMEM((3, 2) + chunk, BF16),
+        pltpu.VMEM(chunk, BF16),
+        pltpu.VMEM((2, 2) + chunk, BF16),
+        pltpu.VMEM((2, 2) + chunk, BF16),
+        pltpu.VMEM((2,) + chunk, BF16),
+        pltpu.VMEM((2,) + chunk, BF16),
+        pltpu.VMEM((3,) + chunk, BF16),
+        pltpu.SemaphoreType.DMA((5,)),
+        pltpu.SemaphoreType.DMA((5,)),
+        pltpu.SemaphoreType.DMA((SENDS,)),
+        pltpu.SemaphoreType.DMA((SENDS,)),
     ]
-    in_vmem = pl.BlockSpec(memory_space=pltpu.VMEM)
+    in_hbm = pl.BlockSpec(memory_space=pltpu.HBM)
     feature_grad, depth_grad, point_grad, bias_grad = pl.pallas_call(
         functools.partial(whole_kernel, images),
         out_shape=(
             jax.ShapeDtypeStruct((cells, channels), BF16),
-            jax.ShapeDtypeStruct(depth_w.shape, BF16),
+            jax.ShapeDtypeStruct((3, 3, 2, channels), BF16),
             jax.ShapeDtypeStruct(point_w.shape, BF16),
             jax.ShapeDtypeStruct(point_bias.shape, F32),
         ),
-        in_specs=[in_vmem] * 5,
-        out_specs=[in_vmem] * 4,
+        in_specs=[in_hbm] * 5,
+        out_specs=[in_hbm] * 4,
         scratch_shapes=scratch,
         compiler_params=pltpu.CompilerParams(
-            collective_id=0, has_side_effects=True, vmem_limit_bytes=40 * 1024 * 1024
+            collective_id=0, has_side_effects=True, vmem_limit_bytes=56 * 1024 * 1024
         ),
         cost_estimate=pl.CostEstimate(flops=2 * 7 * cells * channels * outputs, bytes_accessed=8000000, transcendentals=0),
-    )(features.reshape(cells, channels), depth_w, point_w, point_bias, cotangent.reshape(cells, 2 * outputs))
-    return feature_grad.reshape(features.shape), depth_grad, point_grad, bias_grad
+    )(features.reshape(cells, channels), jnp.transpose(depth_w, (1, 2, 0, 3)), point_w, point_bias, cotangent.reshape(cells, 2 * outputs))
+    return feature_grad.reshape(features.shape), jnp.transpose(depth_grad, (2, 0, 1, 3)), point_grad, bias_grad
 
 
 def fits_fused(mesh):

time: 60.6 us -> 53.4 us (0.88)
  local copies, waits for them, and re-layouts: 8.16 us -> 4.55 us
  Pallas kernels: 51.5 us -> 48.1 us
    unnamed x13 -> x10, local copies, waits for them, and re-layouts: 8.16 us -> 4.55 us
    pallas_call x1, Pallas kernels: 51.5 us -> 48.1 us  [fused_step(): pl.pallas_call(functools.partial(whole_kernel, images), out_shape=(jax.Sh...]
where the time goes in v2:
time: 53.4 us; the launch traced here: 53.3 us
  Pallas kernels  48.1 us (90%)
  local copies, waits for them, and re-layouts  4.55 us (9%)
  between operations  0.66 us (1%)
    pallas_call x1, Pallas kernels, fused_step(): pl.pallas_call(functools.partial(whole_kernel, images), out_shape=(jax.Sh...  48.1 us
    unnamed x10, local copies, waits for them, and re-layouts  4.55 us

profile of v2, /device:TPU:0, one launch (start us, length us, event | category | flops | bytes accessed | tf_op | source)
XLA Modules:
  0.0 53.3 jit_solution(12238137325728639874)
XLA Ops:
  0.6 48.1 %shard_map.84 = (bf16[432,1152]{1,0:T(8,128)(2,1)}, bf16[3,3,2,1152]{3,2,1,0:T(2,128)(2,1)}, bf16[2,1152,256]{2,1,0:T(8,128)(2,1)}, f32[2,256]{1,0:T(2,128)}) custom-call(bf16[432,1152]{1,0:T(8,128)(2,1)} %bitcast.7, bf16[3,3,2,1152]{3,2,1,0:T(2,128)(2,1)} %bitcast.9, bf16[2,1152,256]{2,1,0:T(8,128)(2,1)} %pw_hbm.1, f32[2,256]{1,0:T(2,128)} %bias_hbm.1, ...), custom_call_target="tpu_custom_call" | custom-call | flops 1783627776 | bytes 8000000 | tf_op jit(solution)/shard_map/pallas_call | solution.py:640
  48.7 0.0 copy-start.1
  48.7 0.0 copy-start
  48.7 2.3 %copy.13 = bf16[1,9,48,1152]{3,2,1,0:T(8,128)(2,1)} copy(bf16[1,9,48,1152]{3,2,1,0:T(8,128)(2,1)} %bitcast.5) | data formatting | bytes 1990656
  51.0 0.0 copy-done.1
  51.0 0.6 %copy.14 = bf16[2,3,3,1152]{3,0,2,1:T(2,128)(2,1)} copy(bf16[2,3,3,1152]{3,0,2,1:T(2,128)(2,1)S(1)} %bitcast.6) | data formatting | bytes 82944
  51.7 0.0 copy-done
  51.7 0.0 copy-start.2
  51.7 1.0 %copy.15 = bf16[2,1152,256]{2,1,0:T(8,128)(2,1)} copy(bf16[2,1152,256]{2,1,0:T(8,128)(2,1)S(1)} %copy-done) | data formatting | bytes 2359296
  52.7 0.0 copy-done.2
  52.7 0.6 %copy.16 = f32[2,256]{1,0:T(2,128)} copy(f32[2,256]{1,0:T(2,128)S(1)} %copy-done.2) | data formatting | bytes 4096
Async XLA Ops:
  48.7 2.4 %copy-start.1 = (bf16[3,3,2,1152]{3,2,1,0:T(2,128)(2,1)S(1)}, bf16[3,3,2,1152]{3,2,1,0:T(2,128)(2,1)}, u32[]{:S(2)}) copy-start(bf16[3,3,2,1152]{3,2,1,0:T(2,128)(2,1)} %get-tuple-element.9) | copy-start | bytes 124420
  48.7 3.0 %copy-start = (bf16[2,1152,256]{2,1,0:T(8,128)(2,1)S(1)}, bf16[2,1152,256]{2,1,0:T(8,128)(2,1)}, u32[]{:S(2)}) copy-start(bf16[2,1152,256]{2,1,0:T(8,128)(2,1)} %get-tuple-element.18) | copy-start | bytes 3538948
  51.7 1.0 %copy-start.2 = (f32[2,256]{1,0:T(2,128)S(1)}, f32[2,256]{1,0:T(2,128)}, u32[]{:S(2)}) copy-start(f32[2,256]{1,0:T(2,128)} %get-tuple-element.19) | copy-start | bytes 6148

commit v3 on v2

--- a/solution.py
+++ b/solution.py
@@ -163,7 +163,7 @@
 CHUNK = 80
 POINT_ROWS = 72
 BULK = 64
-SENDS = 33
+SENDS = 37
 
 
 def ring(e, g):
@@ -293,7 +293,7 @@
     fgrad_ref, dgrad_out, pgrad_out, bgrad_out,
     feat_ref, dw_ref, pw_ref, bias_ref, cot_ref,
     feat_in, cot_in, pg_in, depth_s, pg_a, pg_b, dg_a, dg_b, wide_s, taps_s,
-    acc, cur, fin, r0, bx, bz, by, a1y, a1x, a2x, a2y, a3, load_sem, store_sem, send_sem, recv_sem,
+    acc, cur, fin, r0, in_1y, in_1x, in_2x, in_2y, in_3, load_sem, store_sem, send_sem, recv_sem,
 ):
     dp = lax.axis_index("dp")
     my = lax.axis_index("lon")
@@ -363,14 +363,55 @@
                     total = acc[branch, core, y, x, z].astype(F32) + r0[branch, y, x, z].astype(F32)
                     cur[branch, y, x, z] = total.astype(BF16)
 
-    def settle(branch, extras):
-        total = cur[branch, my, mx, mz].astype(F32)
-        for extra in extras:
-            total = total + extra.astype(F32)
-        fin[branch, core, my, mx, mz] = (total * (1.0 / images)).astype(BF16)
-
     every = slice(None)
     lower, upper = pl.ds(0, 2), pl.ds(2, 2)
+
+    def reduce_1(branch):
+        add_halves(branch)
+        return [
+            send(cur.at[branch, 1 - my, :, lower], in_1y.at[branch], other_y),
+            send(cur.at[branch, :, 1 - mx, upper], in_1x.at[branch], other_x),
+        ]
+
+    def reduce_2(branch):
+        for k in range(2):
+            for z in range(2):
+                add_into((branch, my, k, z), in_1y[branch, k, z])
+                add_into((branch, k, mx, 2 + z), in_1x[branch, k, z])
+        return [
+            send(cur.at[branch, my, 1 - mx, lower], in_2x.at[branch], other_x),
+            send(cur.at[branch, 1 - my, mx, upper], in_2y.at[branch], other_y),
+        ]
+
+    def reduce_3(branch):
+        for z in range(2):
+            add_into((branch, my, mx, z), in_2x[branch, z])
+            add_into((branch, my, mx, 2 + z), in_2y[branch, z])
+        return [
+            send(cur.at[branch, my, mx, lax.rem(mz + k + 1, 4)], in_3.at[branch, k], other_z[k]) for k in range(3)
+        ]
+
+    def gather_1(branch):
+        total = cur[branch, my, mx, mz].astype(F32)
+        for k in range(3):
+            total = total + in_3[branch, k].astype(F32)
+        fin[branch, core, my, mx, mz] = (total * (1.0 / images)).astype(BF16)
+        return [share((branch, core, my, mx, mz), peer) for peer in other_z]
+
+    def gather_2(branch):
+        return [
+            share((branch, core, my, mx, lower), other_x),
+            share((branch, core, my, mx, upper), other_y),
+        ]
+
+    def gather_3(branch):
+        return [
+            share((branch, core, my, every, lower), other_y),
+            share((branch, core, every, mx, upper), other_x),
+        ]
+
+    def gather_4(branch):
+        return [share((branch, core), other_core)]
 
     @pl.loop(0, 9)
     def _(at):
@@ -411,11 +452,9 @@
     small_terms(wide_s, taps_s, pg_b, acc, 1)
     b_step.append(send_half(1, pl.ds(BULK, CHUNK - BULK)))
     finish(b_step)
-    add_halves(1)
-    b_step = [send(cur.at[1, :, 1 - mx], bx, other_x)]
+    b_step = reduce_1(1)
 
     feat_copy.wait()
-    cot_copy.wait()
 
     def cell_rows(g, t):
         return pl.ds((3 * g + t) * 48, 48)
@@ -439,6 +478,10 @@
                     high = high + w[1][e + 1] * src_high + w[0][e + 1] * src_low
                 depth_s[cell_rows(g, t), lanes] = join_rows(low, high).astype(BF16)
 
+    finish(b_step)
+    b_step = reduce_2(1)
+
+    cot_copy.wait()
     for g in range(3):
         rows = pl.ds(144 * g, 144)
         upstream = cot_in[...] if g == 2 else cot_ref[pl.ds(288 * g, 144), 0:256]
@@ -446,16 +489,14 @@
     pg_copy = send(pg_a, pg_in, other_y)
 
     finish(b_step)
-
-    @pl.loop(0, 4)
-    def _(z):
-        for y in range(2):
-            add_into((1, y, mx, z), bx[y, z])
-
-    b_step = [send(cur.at[1, :, mx, lax.rem(mz + k + 1, 4)], bz.at[k], other_z[k]) for k in range(3)]
+    b_step = reduce_3(1)
 
     point_terms(depth_s, pg_a, wide_s, acc, 0)
     a_step = [send_half(0, pl.ds(0, BULK))]
+
+    finish(b_step)
+    b_step = gather_1(1)
+
     spread_back(pg_a, pw_ref, 0, dg_a)
 
     @pl.loop(0, 9)
@@ -480,23 +521,10 @@
     a_step.append(send_half(0, pl.ds(BULK, CHUNK - BULK)))
 
     finish(b_step)
-    for y in range(2):
-        total = cur[1, y, mx, mz].astype(F32)
-        for k in range(3):
-            total = total + bz[k, y].astype(F32)
-        cur[1, y, mx, mz] = total.astype(BF16)
-    b_step = [send(cur.at[1, 1 - my, mx, mz], by, other_y)]
+    b_step = gather_2(1)
 
     finish(a_step)
-    add_halves(0)
-    a_step = [
-        send(cur.at[0, 1 - my, :, lower], a1y, other_y),
-        send(cur.at[0, :, 1 - mx, upper], a1x, other_x),
-    ]
-
-    finish(b_step)
-    settle(1, [by[...]])
-    b_step = [share((1, core, my, mx, mz), other_y)]
+    a_step = reduce_1(0)
 
     def branch_b_grad(rows, lanes, w):
         grad = dg_b[rows, lanes].astype(F32)
@@ -526,17 +554,10 @@
                 fgrad_ref[rows, lanes] = total.astype(BF16)
 
     finish(b_step)
-    b_step = [share((1, core, every, mx, mz), peer) for peer in other_z]
+    b_step = gather_3(1)
 
     finish(a_step)
-    for k in range(2):
-        for z in range(2):
-            add_into((0, my, k, z), a1y[k, z])
-            add_into((0, k, mx, 2 + z), a1x[k, z])
-    a_step = [
-        send(cur.at[0, my, 1 - mx, lower], a2x, other_x),
-        send(cur.at[0, 1 - my, mx, upper], a2y, other_y),
-    ]
+    a_step = reduce_2(0)
 
     pg_copy.wait()
     spread_back(pg_in, pw_ref, 0, dg_a)
@@ -555,38 +576,24 @@
     store(fgrad_ref, fgrad_hbm)
 
     finish(a_step)
-    for z in range(2):
-        add_into((0, my, mx, z), a2x[z])
-        add_into((0, my, mx, 2 + z), a2y[z])
-    a_step = [send(cur.at[0, my, mx, lax.rem(mz + k + 1, 4)], a3.at[k], other_z[k]) for k in range(3)]
-
-    finish(b_step)
-    b_step = [share((1, core, every, mx), other_x)]
+    a_step = reduce_3(0)
+
+    finish(b_step)
+    b_step = gather_4(1)
 
     finish(a_step)
-    settle(0, [a3[k] for k in range(3)])
-    a_step = [share((0, core, my, mx, mz), peer) for peer in other_z]
-
-    finish(b_step)
-    b_step = [share((1, core), other_core)]
-
-    finish(a_step)
-    a_step = [
-        share((0, core, my, mx, lower), other_x),
-        share((0, core, my, mx, upper), other_y),
-    ]
+    a_step = gather_1(0)
 
     finish(b_step)
     store_results(fin, 1, pgrad_out, bgrad_out)
     store(pgrad_out.at[1], pgrad_hbm.at[1])
 
     finish(a_step)
-    a_step = [
-        share((0, core, my, every, lower), other_y),
-        share((0, core, every, mx, upper), other_x),
-    ]
+    a_step = gather_2(0)
     finish(a_step)
-    finish([share((0, core), other_core)])
+    a_step = gather_3(0)
+    finish(a_step)
+    finish(gather_4(0))
     store_results(fin, 0, pgrad_out, bgrad_out)
     store(pgrad_out.at[0], pgrad_hbm.at[0])
     store(bgrad_out, bgrad_hbm)
@@ -623,14 +630,11 @@
         pltpu.VMEM((2, 2, 2, 4) + chunk, BF16),
         pltpu.VMEM((2, 2, 2, 2, 4) + chunk, BF16),
         pltpu.VMEM((2, 2, 2, 4) + chunk, BF16),
-        pltpu.VMEM((2, 4) + chunk, BF16),
-        pltpu.VMEM((3, 2) + chunk, BF16),
-        pltpu.VMEM(chunk, BF16),
+        pltpu.VMEM((2, 2, 2) + chunk, BF16),
+        pltpu.VMEM((2, 2, 2) + chunk, BF16),
         pltpu.VMEM((2, 2) + chunk, BF16),
         pltpu.VMEM((2, 2) + chunk, BF16),
-        pltpu.VMEM((2,) + chunk, BF16),
-        pltpu.VMEM((2,) + chunk, BF16),
-        pltpu.VMEM((3,) + chunk, BF16),
+        pltpu.VMEM((2, 3) + chunk, BF16),
         pltpu.SemaphoreType.DMA((5,)),
         pltpu.SemaphoreType.DMA((5,)),
         pltpu.SemaphoreType.DMA((SENDS,)),

time: 53.4 us -> 59.6 us (1.12)
  Pallas kernels: 48.1 us -> 54.3 us
    pallas_call x1, Pallas kernels: 48.1 us -> 54.3 us  [fused_step(): pl.pallas_call(functools.partial(whole_kernel, images), out_shape=(jax.Sh...]
where the time goes in v3:
time: 59.6 us; the launch traced here: 59.5 us
  Pallas kernels  54.3 us (91%)
  local copies, waits for them, and re-layouts  4.55 us (8%)
  between operations  0.66 us (1%)
    pallas_call x1, Pallas kernels, fused_step(): pl.pallas_call(functools.partial(whole_kernel, images), out_shape=(jax.Sh...  54.3 us
    unnamed x10, local copies, waits for them, and re-layouts  4.55 us

profile of v3, /device:TPU:0, one launch (start us, length us, event | category | flops | bytes accessed | tf_op | source)
XLA Modules:
  0.0 59.5 jit_solution(18439694866773371437)
XLA Ops:
  0.6 54.3 %shard_map.84 = (bf16[432,1152]{1,0:T(8,128)(2,1)}, bf16[3,3,2,1152]{3,2,1,0:T(2,128)(2,1)}, bf16[2,1152,256]{2,1,0:T(8,128)(2,1)}, f32[2,256]{1,0:T(2,128)}) custom-call(bf16[432,1152]{1,0:T(8,128)(2,1)} %bitcast.7, bf16[3,3,2,1152]{3,2,1,0:T(2,128)(2,1)} %bitcast.9, bf16[2,1152,256]{2,1,0:T(8,128)(2,1)} %pw_hbm.1, f32[2,256]{1,0:T(2,128)} %bias_hbm.1, ...), custom_call_target="tpu_custom_call" | custom-call | flops 1783627776 | bytes 8000000 | tf_op jit(solution)/shard_map/pallas_call | solution.py:644
  54.9 0.0 copy-start.1
  54.9 0.0 copy-start
  54.9 2.3 %copy.13 = bf16[1,9,48,1152]{3,2,1,0:T(8,128)(2,1)} copy(bf16[1,9,48,1152]{3,2,1,0:T(8,128)(2,1)} %bitcast.5) | data formatting | bytes 1990656
  57.3 0.0 copy-done.1
  57.3 0.6 %copy.14 = bf16[2,3,3,1152]{3,0,2,1:T(2,128)(2,1)} copy(bf16[2,3,3,1152]{3,0,2,1:T(2,128)(2,1)S(1)} %bitcast.6) | data formatting | bytes 82944
  57.9 0.0 copy-done
  57.9 0.0 copy-start.2
  57.9 1.0 %copy.15 = bf16[2,1152,256]{2,1,0:T(8,128)(2,1)} copy(bf16[2,1152,256]{2,1,0:T(8,128)(2,1)S(1)} %copy-done) | data formatting | bytes 2359296
  58.9 0.0 copy-done.2
  58.9 0.6 copy.16
Async XLA Ops:
  54.9 2.4 %copy-start.1 = (bf16[3,3,2,1152]{3,2,1,0:T(2,128)(2,1)S(1)}, bf16[3,3,2,1152]{3,2,1,0:T(2,128)(2,1)}, u32[]{:S(2)}) copy-start(bf16[3,3,2,1152]{3,2,1,0:T(2,128)(2,1)} %get-tuple-element.9) | copy-start | bytes 124420
  54.9 3.0 %copy-start = (bf16[2,1152,256]{2,1,0:T(8,128)(2,1)S(1)}, bf16[2,1152,256]{2,1,0:T(8,128)(2,1)}, u32[]{:S(2)}) copy-start(bf16[2,1152,256]{2,1,0:T(8,128)(2,1)} %get-tuple-element.18) | copy-start | bytes 3538948
  57.9 1.0 %copy-start.2 = (f32[2,256]{1,0:T(2,128)S(1)}, f32[2,256]{1,0:T(2,128)}, u32[]{:S(2)}) copy-start(f32[2,256]{1,0:T(2,128)} %get-tuple-element.19) | copy-start | bytes 6148

commit v4 on v3

--- a/solution.py
+++ b/solution.py
@@ -163,7 +163,7 @@
 CHUNK = 80
 POINT_ROWS = 72
 BULK = 64
-SENDS = 37
+SENDS = 42
 
 
 def ring(e, g):
@@ -293,7 +293,7 @@
     fgrad_ref, dgrad_out, pgrad_out, bgrad_out,
     feat_ref, dw_ref, pw_ref, bias_ref, cot_ref,
     feat_in, cot_in, pg_in, depth_s, pg_a, pg_b, dg_a, dg_b, wide_s, taps_s,
-    acc, cur, fin, r0, in_1y, in_1x, in_2x, in_2y, in_3, load_sem, store_sem, send_sem, recv_sem,
+    acc, cur, fin, r0, in_all, in_plane, in_z, load_sem, store_sem, send_sem, recv_sem,
 ):
     dp = lax.axis_index("dp")
     my = lax.axis_index("lon")
@@ -302,8 +302,17 @@
     mz = dp // 4
     other_y = {"dp": dp, "lon": 1 - my}
     other_core = {"dp": dp + 1 - 2 * core, "lon": my}
-    other_x = {"dp": dp + 2 - 4 * mx, "lon": my}
     other_z = [{"dp": lax.rem(dp + 4 * step, 16), "lon": my} for step in (1, 2, 3)]
+
+    me = my * 8 + mx * 4 + mz
+
+    def owner(at):
+        y, x, z = place(at)
+        return {"dp": (z * 2 + x) * 2 + core, "lon": y}
+
+    owners = [lax.rem(me + step, 16) for step in range(1, 16)]
+    plane = [(1 - my, mx), (my, 1 - mx), (1 - my, 1 - mx)]
+    plane_peers = [{"dp": (mz * 2 + x) * 2 + core, "lon": y} for y, x in plane]
 
     loads = [
         pltpu.make_async_copy(src, dst, load_sem.at[at])
@@ -315,9 +324,9 @@
         copy.start()
 
     barrier = pltpu.get_barrier_semaphore()
-    for peer in [other_y, other_core, other_x] + other_z:
+    for peer in [owner(at) for at in owners] + [other_core]:
         pl.semaphore_signal(barrier, inc=1, device_id=peer, device_id_type=MESH)
-    pl.semaphore_wait(barrier, 6)
+    pl.semaphore_wait(barrier, 16)
 
     numbers = iter(range(SENDS))
 
@@ -346,9 +355,6 @@
     finish(loads)
     taps_s[...] = jnp.zeros_like(taps_s)
 
-    def add_into(at, extra):
-        cur[at] = (cur[at].astype(F32) + extra.astype(F32)).astype(BF16)
-
     def share(index, peer):
         return send(fin.at[index], fin.at[index], peer)
 
@@ -363,54 +369,41 @@
                     total = acc[branch, core, y, x, z].astype(F32) + r0[branch, y, x, z].astype(F32)
                     cur[branch, y, x, z] = total.astype(BF16)
 
-    every = slice(None)
-    lower, upper = pl.ds(0, 2), pl.ds(2, 2)
-
-    def reduce_1(branch):
+    def scatter_all(branch):
+        add_halves(branch)
+        return [send(cur.at[(branch,) + place(at)], in_all.at[k], owner(at)) for k, at in enumerate(owners)]
+
+    def scatter_plane(branch):
         add_halves(branch)
         return [
-            send(cur.at[branch, 1 - my, :, lower], in_1y.at[branch], other_y),
-            send(cur.at[branch, :, 1 - mx, upper], in_1x.at[branch], other_x),
+            send(cur.at[branch, y, x], in_plane.at[k], peer) for k, ((y, x), peer) in enumerate(zip(plane, plane_peers))
         ]
 
-    def reduce_2(branch):
-        for k in range(2):
-            for z in range(2):
-                add_into((branch, my, k, z), in_1y[branch, k, z])
-                add_into((branch, k, mx, 2 + z), in_1x[branch, k, z])
+    def scatter_z(branch):
+        @pl.loop(0, 4)
+        def _(z):
+            total = cur[branch, my, mx, z].astype(F32)
+            for k in range(3):
+                total = total + in_plane[k, z].astype(F32)
+            cur[branch, my, mx, z] = total.astype(BF16)
+
         return [
-            send(cur.at[branch, my, 1 - mx, lower], in_2x.at[branch], other_x),
-            send(cur.at[branch, 1 - my, mx, upper], in_2y.at[branch], other_y),
+            send(cur.at[branch, my, mx, lax.rem(mz + k + 1, 4)], in_z.at[k], other_z[k]) for k in range(3)
         ]
 
-    def reduce_3(branch):
-        for z in range(2):
-            add_into((branch, my, mx, z), in_2x[branch, z])
-            add_into((branch, my, mx, 2 + z), in_2y[branch, z])
-        return [
-            send(cur.at[branch, my, mx, lax.rem(mz + k + 1, 4)], in_3.at[branch, k], other_z[k]) for k in range(3)
-        ]
-
-    def gather_1(branch):
+    def settle(branch, arrived):
         total = cur[branch, my, mx, mz].astype(F32)
-        for k in range(3):
-            total = total + in_3[branch, k].astype(F32)
+        for k in range(arrived.shape[0]):
+            total = total + arrived[k].astype(F32)
         fin[branch, core, my, mx, mz] = (total * (1.0 / images)).astype(BF16)
+
+    def gather_z(branch):
         return [share((branch, core, my, mx, mz), peer) for peer in other_z]
 
-    def gather_2(branch):
-        return [
-            share((branch, core, my, mx, lower), other_x),
-            share((branch, core, my, mx, upper), other_y),
-        ]
-
-    def gather_3(branch):
-        return [
-            share((branch, core, my, every, lower), other_y),
-            share((branch, core, every, mx, upper), other_x),
-        ]
-
-    def gather_4(branch):
+    def gather_plane(branch):
+        return [share((branch, core, my, mx), peer) for peer in plane_peers]
+
+    def gather_core(branch):
         return [share((branch, core), other_core)]
 
     @pl.loop(0, 9)
@@ -451,10 +444,10 @@
 
     small_terms(wide_s, taps_s, pg_b, acc, 1)
     b_step.append(send_half(1, pl.ds(BULK, CHUNK - BULK)))
+
+    feat_copy.wait()
     finish(b_step)
-    b_step = reduce_1(1)
-
-    feat_copy.wait()
+    b_step = scatter_all(1)
 
     def cell_rows(g, t):
         return pl.ds((3 * g + t) * 48, 48)
@@ -478,9 +471,6 @@
                     high = high + w[1][e + 1] * src_high + w[0][e + 1] * src_low
                 depth_s[cell_rows(g, t), lanes] = join_rows(low, high).astype(BF16)
 
-    finish(b_step)
-    b_step = reduce_2(1)
-
     cot_copy.wait()
     for g in range(3):
         rows = pl.ds(144 * g, 144)
@@ -488,15 +478,8 @@
         pg_a[rows, :] = point_step(depth_s[rows, :], pw_ref[0], bias_ref[0:1, :], upstream)
     pg_copy = send(pg_a, pg_in, other_y)
 
-    finish(b_step)
-    b_step = reduce_3(1)
-
     point_terms(depth_s, pg_a, wide_s, acc, 0)
     a_step = [send_half(0, pl.ds(0, BULK))]
-
-    finish(b_step)
-    b_step = gather_1(1)
-
     spread_back(pg_a, pw_ref, 0, dg_a)
 
     @pl.loop(0, 9)
@@ -521,10 +504,11 @@
     a_step.append(send_half(0, pl.ds(BULK, CHUNK - BULK)))
 
     finish(b_step)
-    b_step = gather_2(1)
+    settle(1, in_all)
+    b_step = gather_z(1)
 
     finish(a_step)
-    a_step = reduce_1(0)
+    a_step = scatter_plane(0)
 
     def branch_b_grad(rows, lanes, w):
         grad = dg_b[rows, lanes].astype(F32)
@@ -553,11 +537,11 @@
                 total = branch_a_grad(w, grads, g) + branch_b_grad(rows, lanes, wb)
                 fgrad_ref[rows, lanes] = total.astype(BF16)
 
+    finish(a_step)
+    a_step = scatter_z(0)
+
     finish(b_step)
-    b_step = gather_3(1)
-
-    finish(a_step)
-    a_step = reduce_2(0)
+    b_step = gather_plane(1)
 
     pg_copy.wait()
     spread_back(pg_in, pw_ref, 0, dg_a)
@@ -576,24 +560,21 @@
     store(fgrad_ref, fgrad_hbm)
 
     finish(a_step)
-    a_step = reduce_3(0)
+    settle(0, in_z)
+    a_step = gather_z(0)
 
     finish(b_step)
-    b_step = gather_4(1)
+    b_step = gather_core(1)
 
     finish(a_step)
-    a_step = gather_1(0)
+    a_step = gather_plane(0)
 
     finish(b_step)
     store_results(fin, 1, pgrad_out, bgrad_out)
     store(pgrad_out.at[1], pgrad_hbm.at[1])
 
     finish(a_step)
-    a_step = gather_2(0)
-    finish(a_step)
-    a_step = gather_3(0)
-    finish(a_step)
-    finish(gather_4(0))
+    finish(gather_core(0))
     store_results(fin, 0, pgrad_out, bgrad_out)
     store(pgrad_out.at[0], pgrad_hbm.at[0])
     store(bgrad_out, bgrad_hbm)
@@ -630,11 +611,9 @@
         pltpu.VMEM((2, 2, 2, 4) + chunk, BF16),
         pltpu.VMEM((2, 2, 2, 2, 4) + chunk, BF16),
         pltpu.VMEM((2, 2, 2, 4) + chunk, BF16),
-        pltpu.VMEM((2, 2, 2) + chunk, BF16),
-        pltpu.VMEM((2, 2, 2) + chunk, BF16),
-        pltpu.VMEM((2, 2) + chunk, BF16),
-        pltpu.VMEM((2, 2) + chunk, BF16),
-        pltpu.VMEM((2, 3) + chunk, BF16),
+        pltpu.VMEM((15,) + chunk, BF16),
+        pltpu.VMEM((3, 4) + chunk, BF16),
+        pltpu.VMEM((3,) + chunk, BF16),
         pltpu.SemaphoreType.DMA((5,)),
         pltpu.SemaphoreType.DMA((5,)),
         pltpu.SemaphoreType.DMA((SENDS,)),

time: 59.6 us -> 52.4 us (0.88)
  Pallas kernels: 54.3 us -> 47 us
    pallas_call x1, Pallas kernels: 54.3 us -> 47 us  [fused_step(): pl.pallas_call(functools.partial(whole_kernel, images), out_shape=(jax.Sh...]
where the time goes in v4:
time: 52.4 us; the launch traced here: 52.2 us
  Pallas kernels  47 us (90%)
  local copies, waits for them, and re-layouts  4.55 us (9%)
  between operations  0.66 us (1%)
    pallas_call x1, Pallas kernels, fused_step(): pl.pallas_call(functools.partial(whole_kernel, images), out_shape=(jax.Sh...  47 us
    unnamed x10, local copies, waits for them, and re-layouts  4.55 us

profile of v4, /device:TPU:0, one launch (start us, length us, event | category | flops | bytes accessed | tf_op | source)
XLA Modules:
  0.0 52.2 jit_solution(3438087827695984002)
XLA Ops:
  0.6 47.0 %shard_map.84 = (bf16[432,1152]{1,0:T(8,128)(2,1)}, bf16[3,3,2,1152]{3,2,1,0:T(2,128)(2,1)}, bf16[2,1152,256]{2,1,0:T(8,128)(2,1)}, f32[2,256]{1,0:T(2,128)}) custom-call(bf16[432,1152]{1,0:T(8,128)(2,1)} %bitcast.7, bf16[3,3,2,1152]{3,2,1,0:T(2,128)(2,1)} %bitcast.9, bf16[2,1152,256]{2,1,0:T(8,128)(2,1)} %pw_hbm.1, f32[2,256]{1,0:T(2,128)} %bias_hbm.1, ...), custom_call_target="tpu_custom_call" | custom-call | flops 1783627776 | bytes 8000000 | tf_op jit(solution)/shard_map/pallas_call | solution.py:623
  47.6 0.0 copy-start.1
  47.6 0.0 copy-start
  47.7 2.3 %copy.13 = bf16[1,9,48,1152]{3,2,1,0:T(8,128)(2,1)} copy(bf16[1,9,48,1152]{3,2,1,0:T(8,128)(2,1)} %bitcast.5) | data formatting | bytes 1990656
  50.0 0.0 copy-done.1
  50.0 0.6 %copy.14 = bf16[2,3,3,1152]{3,0,2,1:T(2,128)(2,1)} copy(bf16[2,3,3,1152]{3,0,2,1:T(2,128)(2,1)S(1)} %bitcast.6) | data formatting | bytes 82944
  50.6 0.0 copy-done
  50.6 0.0 copy-start.2
  50.6 1.0 %copy.15 = bf16[2,1152,256]{2,1,0:T(8,128)(2,1)} copy(bf16[2,1152,256]{2,1,0:T(8,128)(2,1)S(1)} %copy-done) | data formatting | bytes 2359296
  51.6 0.0 copy-done.2
  51.6 0.6 %copy.16 = f32[2,256]{1,0:T(2,128)} copy(f32[2,256]{1,0:T(2,128)S(1)} %copy-done.2) | data formatting | bytes 4096
Async XLA Ops:
  47.6 2.4 %copy-start.1 = (bf16[3,3,2,1152]{3,2,1,0:T(2,128)(2,1)S(1)}, bf16[3,3,2,1152]{3,2,1,0:T(2,128)(2,1)}, u32[]{:S(2)}) copy-start(bf16[3,3,2,1152]{3,2,1,0:T(2,128)(2,1)} %get-tuple-element.9) | copy-start | bytes 124420
  47.6 3.0 %copy-start = (bf16[2,1152,256]{2,1,0:T(8,128)(2,1)S(1)}, bf16[2,1152,256]{2,1,0:T(8,128)(2,1)}, u32[]{:S(2)}) copy-start(bf16[2,1152,256]{2,1,0:T(8,128)(2,1)} %get-tuple-element.18) | copy-start | bytes 3538948
  50.6 1.0 %copy-start.2 = (f32[2,256]{1,0:T(2,128)S(1)}, f32[2,256]{1,0:T(2,128)}, u32[]{:S(2)}) copy-start(f32[2,256]{1,0:T(2,128)} %get-tuple-element.19) | copy-start | bytes 6148

commit v5 on v4

--- a/solution.py
+++ b/solution.py
@@ -163,7 +163,7 @@
 CHUNK = 80
 POINT_ROWS = 72
 BULK = 64
-SENDS = 42
+SENDS = 55
 
 
 def ring(e, g):
@@ -361,50 +361,55 @@
     def send_half(branch, rows):
         return send(acc.at[branch, 1 - core, :, :, :, rows], r0.at[branch, :, :, :, rows], other_core)
 
-    def add_halves(branch):
+    whole_rows, bulk_rows, tail_rows = pl.ds(0, CHUNK), pl.ds(0, BULK), pl.ds(BULK, CHUNK - BULK)
+
+    def add_halves(branch, rows):
         @pl.loop(0, 4)
         def _(z):
             for y in range(2):
                 for x in range(2):
-                    total = acc[branch, core, y, x, z].astype(F32) + r0[branch, y, x, z].astype(F32)
-                    cur[branch, y, x, z] = total.astype(BF16)
+                    total = acc[branch, core, y, x, z, rows].astype(F32) + r0[branch, y, x, z, rows].astype(F32)
+                    cur[branch, y, x, z, rows] = total.astype(BF16)
 
     def scatter_all(branch):
-        add_halves(branch)
+        add_halves(branch, whole_rows)
         return [send(cur.at[(branch,) + place(at)], in_all.at[k], owner(at)) for k, at in enumerate(owners)]
 
-    def scatter_plane(branch):
-        add_halves(branch)
+    def scatter_plane(branch, rows):
+        add_halves(branch, rows)
         return [
-            send(cur.at[branch, y, x], in_plane.at[k], peer) for k, ((y, x), peer) in enumerate(zip(plane, plane_peers))
+            send(cur.at[branch, y, x, :, rows], in_plane.at[k, :, rows], peer)
+            for k, ((y, x), peer) in enumerate(zip(plane, plane_peers))
         ]
 
-    def scatter_z(branch):
+    def scatter_z(branch, rows):
         @pl.loop(0, 4)
         def _(z):
-            total = cur[branch, my, mx, z].astype(F32)
+            total = cur[branch, my, mx, z, rows].astype(F32)
             for k in range(3):
-                total = total + in_plane[k, z].astype(F32)
-            cur[branch, my, mx, z] = total.astype(BF16)
+                total = total + in_plane[k, z, rows].astype(F32)
+            cur[branch, my, mx, z, rows] = total.astype(BF16)
 
         return [
-            send(cur.at[branch, my, mx, lax.rem(mz + k + 1, 4)], in_z.at[k], other_z[k]) for k in range(3)
+            send(cur.at[branch, my, mx, lax.rem(mz + k + 1, 4), rows], in_z.at[k, rows], other_z[k]) for k in range(3)
         ]
 
-    def settle(branch, arrived):
-        total = cur[branch, my, mx, mz].astype(F32)
+    def settle(branch, arrived, rows):
+        total = cur[branch, my, mx, mz, rows].astype(F32)
         for k in range(arrived.shape[0]):
-            total = total + arrived[k].astype(F32)
-        fin[branch, core, my, mx, mz] = (total * (1.0 / images)).astype(BF16)
-
-    def gather_z(branch):
-        return [share((branch, core, my, mx, mz), peer) for peer in other_z]
-
-    def gather_plane(branch):
-        return [share((branch, core, my, mx), peer) for peer in plane_peers]
-
-    def gather_core(branch):
-        return [share((branch, core), other_core)]
+            total = total + arrived[k, rows].astype(F32)
+        fin[branch, core, my, mx, mz, rows] = (total * (1.0 / images)).astype(BF16)
+
+    every = slice(None)
+
+    def gather_z(branch, rows):
+        return [share((branch, core, my, mx, mz, rows), peer) for peer in other_z]
+
+    def gather_plane(branch, rows):
+        return [share((branch, core, my, mx, every, rows), peer) for peer in plane_peers]
+
+    def gather_core(branch, rows):
+        return [share((branch, core, every, every, every, rows), other_core)]
 
     @pl.loop(0, 9)
     def _(at):
@@ -482,6 +487,9 @@
     a_step = [send_half(0, pl.ds(0, BULK))]
     spread_back(pg_a, pw_ref, 0, dg_a)
 
+    finish(a_step)
+    a_step = scatter_plane(0, bulk_rows)
+
     @pl.loop(0, 9)
     def _(at):
         lanes = lane_block(at)
@@ -501,14 +509,16 @@
                 taps_s[tap // 8, at, tap % 8 : tap % 8 + 1, :] = jnp.sum(sums[a][e], axis=0, keepdims=True)
 
     small_terms(wide_s, taps_s, pg_a, acc, 0)
-    a_step.append(send_half(0, pl.ds(BULK, CHUNK - BULK)))
+    a_tail = [send_half(0, tail_rows)]
 
     finish(b_step)
-    settle(1, in_all)
-    b_step = gather_z(1)
+    settle(1, in_all, whole_rows)
+    b_step = gather_z(1, whole_rows)
 
     finish(a_step)
-    a_step = scatter_plane(0)
+    a_step = scatter_z(0, bulk_rows)
+    finish(a_tail)
+    a_tail = scatter_plane(0, tail_rows)
 
     def branch_b_grad(rows, lanes, w):
         grad = dg_b[rows, lanes].astype(F32)
@@ -538,10 +548,13 @@
                 fgrad_ref[rows, lanes] = total.astype(BF16)
 
     finish(a_step)
-    a_step = scatter_z(0)
+    settle(0, in_z, bulk_rows)
+    a_step = gather_z(0, bulk_rows)
+    finish(a_tail)
+    a_tail = scatter_z(0, tail_rows)
 
     finish(b_step)
-    b_step = gather_plane(1)
+    b_step = gather_plane(1, whole_rows)
 
     pg_copy.wait()
     spread_back(pg_in, pw_ref, 0, dg_a)
@@ -560,21 +573,27 @@
     store(fgrad_ref, fgrad_hbm)
 
     finish(a_step)
-    settle(0, in_z)
-    a_step = gather_z(0)
+    a_step = gather_plane(0, bulk_rows)
+    finish(a_tail)
+    settle(0, in_z, tail_rows)
+    a_tail = gather_z(0, tail_rows)
 
     finish(b_step)
-    b_step = gather_core(1)
-
+    b_step = gather_core(1, whole_rows)
+
+    finish(a_tail)
+    a_tail = gather_plane(0, tail_rows)
     finish(a_step)
-    a_step = gather_plane(0)
+    a_step = gather_core(0, bulk_rows)
 
     finish(b_step)
     store_results(fin, 1, pgrad_out, bgrad_out)
     store(pgrad_out.at[1], pgrad_hbm.at[1])
 
+    finish(a_tail)
+    a_tail = gather_core(0, tail_rows)
     finish(a_step)
-    finish(gather_core(0))
+    finish(a_tail)
     store_results(fin, 0, pgrad_out, bgrad_out)
     store(pgrad_out.at[0], pgrad_hbm.at[0])
     store(bgrad_out, bgrad_hbm)

time: 52.4 us -> 51.9 us (level)
  no operation moved by 1% of the time
where the time goes in v5:
time: 51.9 us; the launch traced here: 51.8 us
  Pallas kernels  46.6 us (90%)
  local copies, waits for them, and re-layouts  4.55 us (9%)
  between operations  0.66 us (1%)
    pallas_call x1, Pallas kernels, fused_step(): pl.pallas_call(functools.partial(whole_kernel, images), out_shape=(jax.Sh...  46.6 us
    unnamed x10, local copies, waits for them, and re-layouts  4.55 us

profile of v5, /device:TPU:0, one launch (start us, length us, event | category | flops | bytes accessed | tf_op | source)
XLA Modules:
  0.0 51.8 jit_solution(6597516564937358081)
XLA Ops:
  0.6 46.6 %shard_map.84 = (bf16[432,1152]{1,0:T(8,128)(2,1)}, bf16[3,3,2,1152]{3,2,1,0:T(2,128)(2,1)}, bf16[2,1152,256]{2,1,0:T(8,128)(2,1)}, f32[2,256]{1,0:T(2,128)}) custom-call(bf16[432,1152]{1,0:T(8,128)(2,1)} %bitcast.7, bf16[3,3,2,1152]{3,2,1,0:T(2,128)(2,1)} %bitcast.9, bf16[2,1152,256]{2,1,0:T(8,128)(2,1)} %pw_hbm.1, f32[2,256]{1,0:T(2,128)} %bias_hbm.1, ...), custom_call_target="tpu_custom_call" | custom-call | flops 1783627776 | bytes 8000000 | tf_op jit(solution)/shard_map/pallas_call | solution.py:642
  47.2 0.0 copy-start.1
  47.2 0.0 copy-start
  47.2 2.3 %copy.13 = bf16[1,9,48,1152]{3,2,1,0:T(8,128)(2,1)} copy(bf16[1,9,48,1152]{3,2,1,0:T(8,128)(2,1)} %bitcast.5) | data formatting | bytes 1990656
  49.5 0.0 copy-done.1
  49.6 0.6 %copy.14 = bf16[2,3,3,1152]{3,0,2,1:T(2,128)(2,1)} copy(bf16[2,3,3,1152]{3,0,2,1:T(2,128)(2,1)S(1)} %bitcast.6) | data formatting | bytes 82944
  50.2 0.0 copy-done
  50.2 0.0 copy-start.2
  50.2 1.0 %copy.15 = bf16[2,1152,256]{2,1,0:T(8,128)(2,1)} copy(bf16[2,1152,256]{2,1,0:T(8,128)(2,1)S(1)} %copy-done) | data formatting | bytes 2359296
  51.2 0.0 copy-done.2
  51.2 0.6 %copy.16 = f32[2,256]{1,0:T(2,128)} copy(f32[2,256]{1,0:T(2,128)S(1)} %copy-done.2) | data formatting | bytes 4096
Async XLA Ops:
  47.2 2.4 %copy-start.1 = (bf16[3,3,2,1152]{3,2,1,0:T(2,128)(2,1)S(1)}, bf16[3,3,2,1152]{3,2,1,0:T(2,128)(2,1)}, u32[]{:S(2)}) copy-start(bf16[3,3,2,1152]{3,2,1,0:T(2,128)(2,1)} %get-tuple-element.9) | copy-start | bytes 124420
  47.2 3.0 %copy-start = (bf16[2,1152,256]{2,1,0:T(8,128)(2,1)S(1)}, bf16[2,1152,256]{2,1,0:T(8,128)(2,1)}, u32[]{:S(2)}) copy-start(bf16[2,1152,256]{2,1,0:T(8,128)(2,1)} %get-tuple-element.18) | copy-start | bytes 3538948
  50.2 1.0 %copy-start.2 = (f32[2,256]{1,0:T(2,128)S(1)}, f32[2,256]{1,0:T(2,128)}, u32[]{:S(2)}) copy-start(f32[2,256]{1,0:T(2,128)} %get-tuple-element.19) | copy-start | bytes 6148
